TPU v7x, 512 devices: a whole 4x4x16 slice. The times are simulated.
512 devices in a mesh: tm: 16 (over z), space: 32 (over x, y, core).
Axes of the slice: x: 4, y: 4, z: 16, core: 2. Of those that a mesh axis runs over, the one named last changes fastest.
Arguments:
- starts: float32 [16, 512, 4096], P('tm', 'space'), may hold values from -15 to 15
- kappa: float32 [512, 4096], P('space'), may hold values from 0.5 to 4
- velocity_x: float32 [512, 4096], P('space'), may hold values from -0.8 to 0.8
- velocity_y: float32 [512, 4096], P('space'), may hold values from -0.8 to 0.8
Outputs:
- corrected: float32 [16, 512, 4096], P('tm', 'space')
All inputs are finite; a program needn't handle non-finite values.
Results may differ from a plain program's by a relative error of at most 0.0003.
Values sent between devices are 32-bit elements; how exact they have to be, the bound alone decides.
No kernel may reach another device: no remote copies, remote signals or barrier semaphores. Data moves between devices by JAX's collectives and lax.ppermute only.
A program may use at most 64 MiB of HBM per device.

v0:
```python
import math

import jax
import jax.numpy as jnp
from jax import lax
from jax.sharding import PartitionSpec as P

STEPS = 2
SWEEPS = 8


step_tau = 0.4


def with_halo(array, sides, width):
    for axis, dim in sides:
        peers, length = (lax.axis_size(axis), array.shape[dim])
        up = [(i, (i + 1) % peers) for i in range(peers - 1)]
        down = [(j, i) for i, j in up]
        last = lax.slice_in_dim(array, length - width, length, axis=dim)
        leading = lax.slice_in_dim(array, 0, width, axis=dim)
        before = lax.ppermute(last, axis, up)
        after = lax.ppermute(leading, axis, down)
        array = jnp.concatenate([before, array, after], axis=dim)
    return array


def chebyshev_weights(sweep_count):
    return [
        1.0 / (1.0 - 0.8 * math.cos(math.pi * (2 * order + 1) / (2.0 * sweep_count)))
        for order in range(sweep_count)
    ]


def face_weights(kappa_pad):
    center = kappa_pad[1:-1, 1:-1]
    north_face = 0.5 * (center + kappa_pad[:-2, 1:-1])
    south_face = 0.5 * (center + kappa_pad[2:, 1:-1])
    west_face = 0.5 * (center + kappa_pad[1:-1, :-2])
    east_face = 0.5 * (center + kappa_pad[1:-1, 2:])
    return (north_face, south_face, west_face, east_face)


def apply_operator(padded, faces, diagonal, velocity_x, velocity_y):
    north_face, south_face, west_face, east_face = faces
    center = padded[..., 1:-1, 1:-1]
    north = padded[..., :-2, 1:-1]
    south = padded[..., 2:, 1:-1]
    west = padded[..., 1:-1, :-2]
    east = padded[..., 1:-1, 2:]
    beside = north_face * north + south_face * south + west_face * west + east_face * east
    carried = 0.5 * velocity_x * (east - west) + 0.5 * velocity_y * (south - north)
    return diagonal * center - step_tau * beside + step_tau * carried


def coefficients(gram_matrix, cross_matrix):
    slices_here = gram_matrix.shape[0]
    drift = cross_matrix - gram_matrix
    factor = jnp.linalg.cholesky(gram_matrix)
    step_terms = jnp.concatenate(
        [cross_matrix[:, :-1] - gram_matrix[:, 1:], jnp.zeros((slices_here, 1), gram_matrix.dtype)],
        axis=1,
    )

    def advance(carried, column):
        alpha_now, sigma_sum = carried
        right_side = sigma_sum + jnp.dot(drift, alpha_now, precision=lax.Precision.HIGHEST)
        alpha_next = alpha_now + jax.scipy.linalg.cho_solve((factor, True), right_side)
        return ((alpha_next, sigma_sum + column), alpha_now)

    zero_vec = jnp.zeros((slices_here,), gram_matrix.dtype)
    _, alphas = lax.scan(advance, (zero_vec, zero_vec), step_terms.T)
    order_ids = jnp.arange(slices_here)
    below_mask = jnp.where(order_ids[:, None] < order_ids[None, :], 1.0, 0.0).astype(
        gram_matrix.dtype
    )
    return alphas.T + below_mask


def per_device(starts, kappa, velocity_x, velocity_y):
    own_start = starts[0]
    kappa_rim = with_halo(kappa, (("space", 0),), 1)
    kappa_pad = jnp.pad(kappa_rim, ((0, 0), (1, 1)))
    faces = face_weights(kappa_pad)
    diagonal = 1.0 + step_tau * (faces[0] + faces[1] + faces[2] + faces[3])
    weights = jnp.asarray(chebyshev_weights(SWEEPS), jnp.float32)
    previous = own_start
    current = own_start

    def operate(field_now):
        field_rim = with_halo(field_now, (("space", 0),), 1)
        padded = jnp.pad(field_rim, ((0, 0), (1, 1)))
        return apply_operator(padded, faces, diagonal, velocity_x, velocity_y)

    for time_step in range(STEPS):
        right_side = (4.0 * current - previous) / 3.0

        def relax_once(sweep_index, field_now):
            return field_now + weights[sweep_index] * (right_side - operate(field_now)) / diagonal

        updated = lax.fori_loop(0, SWEEPS, relax_once, current)
        previous, current = (current, updated)
    change = current - own_start
    slice_index = lax.axis_index("tm")
    all_starts, all_changes = (
        lax.all_gather(starts, "tm", axis=0, tiled=True),
        lax.all_gather(change[None], "tm", axis=0, tiled=True),
    )
    all_ends = all_starts + all_changes
    gram_part = jnp.einsum("krc,irc->ki", all_starts, all_starts, precision=lax.Precision.HIGHEST)
    cross_part = jnp.einsum("krc,irc->ki", all_starts, all_ends, precision=lax.Precision.HIGHEST)
    gram_matrix, cross_matrix = lax.psum((gram_part, cross_part), "space")
    mix_weights = coefficients(gram_matrix, cross_matrix)
    target_coefs = lax.dynamic_slice_in_dim(mix_weights, slice_index, 1, 1)[:, 0]
    result = all_starts[0] + jnp.einsum(
        "i,irc->rc", target_coefs, all_changes, precision=lax.Precision.HIGHEST
    )
    return result[None]


def solution(mesh):
    in_specs = (P("tm", "space", None), P("space", None), P("space", None), P("space", None))
    out_specs = P("tm", "space", None)
    return jax.shard_map(
        per_device, mesh=mesh, in_specs=in_specs, out_specs=out_specs, check_vma=False
    )
```

profile of v0, /device:TPU:32, one launch (start us, length us, event | category | flops | bytes accessed | tf_op | source)
XLA Modules:
  0.0 455.4 jit_solution(6912189596924264047)
XLA Ops:
  7.6 1.7 collective-permute-start.4
  9.3 1.3 collective-permute-start.5
  15.0 1.4 multiply_add_fusion
  16.4 66.1 %while.50 = (s32[]{:T(128)}, f32[16,4096]{1,0:T(8,128)S(1)}, f32[16,4096]{1,0:T(8,128)S(1)}, f32[16,4096]{1,0:T(8,128)S(1)}, f32[16,4096]{1,0:T(8,128)S(1)}, /*i...) while((s32[]{:T(128)}, f32[16,4096]{1,0:T(8,128)S(1)}, ...), condition=%wide.region_1.2_spmd.clone.clone, body=%wide.region_0.1_spmd.sunk.clone.sunk.clone | while | flops 2228514 | bytes 4489565 | solution.py:101
  16.5 1.3 collective-permute-start
  17.8 5.0 %collective-permute-start.1 = (f32[1,4096]{1,0:T(1,128)S(1)}, f32[1,4096]{1,0:T(1,128)S(1)}, u32[]{:S(2)}, u32[]{:S(2)}) collective-permute-start(f32[1,4096]{1,0:T(1,128)S(1)} %get-tuple-element.937), channel_id=1, source_target_pairs={{0,1},{1,2},{2,3},{3,4},{4,5},{5,6},{6,7},{7,8},{8,9},{9,10},{10,1... | collective-permute-start | bytes 49160 | tf_op jit(solution)/shard_map/while/body/eval_jaxpr/ppermute | solution.py:22
  25.0 1.3 collective-permute-start
  26.3 4.3 collective-permute-start.1
  32.7 1.3 collective-permute-start
  34.0 4.9 %collective-permute-start.1 = (f32[1,4096]{1,0:T(1,128)S(1)}, f32[1,4096]{1,0:T(1,128)S(1)}, u32[]{:S(2)}, u32[]{:S(2)}) collective-permute-start(f32[1,4096]{1,0:T(1,128)S(1)} %get-tuple-element.937), channel_id=1, source_target_pairs={{0,1},{1,2},{2,3},{3,4},{4,5},{5,6},{6,7},{7,8},{8,9},{9,10},{10,1... | collective-permute-start | bytes 49160 | tf_op jit(solution)/shard_map/while/body/eval_jaxpr/ppermute | solution.py:22
  41.0 1.3 collective-permute-start
  42.3 4.9 %collective-permute-start.1 = (f32[1,4096]{1,0:T(1,128)S(1)}, f32[1,4096]{1,0:T(1,128)S(1)}, u32[]{:S(2)}, u32[]{:S(2)}) collective-permute-start(f32[1,4096]{1,0:T(1,128)S(1)} %get-tuple-element.937), channel_id=1, source_target_pairs={{0,1},{1,2},{2,3},{3,4},{4,5},{5,6},{6,7},{7,8},{8,9},{9,10},{10,1... | collective-permute-start | bytes 49160 | tf_op jit(solution)/shard_map/while/body/eval_jaxpr/ppermute | solution.py:22
  49.4 1.3 collective-permute-start
  50.7 4.9 %collective-permute-start.1 = (f32[1,4096]{1,0:T(1,128)S(1)}, f32[1,4096]{1,0:T(1,128)S(1)}, u32[]{:S(2)}, u32[]{:S(2)}) collective-permute-start(f32[1,4096]{1,0:T(1,128)S(1)} %get-tuple-element.937), channel_id=1, source_target_pairs={{0,1},{1,2},{2,3},{3,4},{4,5},{5,6},{6,7},{7,8},{8,9},{9,10},{10,1... | collective-permute-start | bytes 49160 | tf_op jit(solution)/shard_map/while/body/eval_jaxpr/ppermute | solution.py:22
  57.7 1.3 collective-permute-start
  59.0 4.9 %collective-permute-start.1 = (f32[1,4096]{1,0:T(1,128)S(1)}, f32[1,4096]{1,0:T(1,128)S(1)}, u32[]{:S(2)}, u32[]{:S(2)}) collective-permute-start(f32[1,4096]{1,0:T(1,128)S(1)} %get-tuple-element.937), channel_id=1, source_target_pairs={{0,1},{1,2},{2,3},{3,4},{4,5},{5,6},{6,7},{7,8},{8,9},{9,10},{10,1... | collective-permute-start | bytes 49160 | tf_op jit(solution)/shard_map/while/body/eval_jaxpr/ppermute | solution.py:22
  66.0 1.3 collective-permute-start
  67.3 4.9 %collective-permute-start.1 = (f32[1,4096]{1,0:T(1,128)S(1)}, f32[1,4096]{1,0:T(1,128)S(1)}, u32[]{:S(2)}, u32[]{:S(2)}) collective-permute-start(f32[1,4096]{1,0:T(1,128)S(1)} %get-tuple-element.937), channel_id=1, source_target_pairs={{0,1},{1,2},{2,3},{3,4},{4,5},{5,6},{6,7},{7,8},{8,9},{9,10},{10,1... | collective-permute-start | bytes 49160 | tf_op jit(solution)/shard_map/while/body/eval_jaxpr/ppermute | solution.py:22
  74.3 1.3 collective-permute-start
  75.6 4.9 %collective-permute-start.1 = (f32[1,4096]{1,0:T(1,128)S(1)}, f32[1,4096]{1,0:T(1,128)S(1)}, u32[]{:S(2)}, u32[]{:S(2)}) collective-permute-start(f32[1,4096]{1,0:T(1,128)S(1)} %get-tuple-element.937), channel_id=1, source_target_pairs={{0,1},{1,2},{2,3},{3,4},{4,5},{5,6},{6,7},{7,8},{8,9},{9,10},{10,1... | collective-permute-start | bytes 49160 | tf_op jit(solution)/shard_map/while/body/eval_jaxpr/ppermute | solution.py:22
  82.6 78.3 %while.51 = (s32[]{:T(128)}, f32[16,4096]{1,0:T(8,128)S(1)}, f32[16,4096]{1,0:T(8,128)S(1)}, f32[16,4096]{1,0:T(8,128)S(1)}, f32[16,4096]{1,0:T(8,128)S(1)}, /*i...) while((s32[]{:T(128)}, f32[16,4096]{1,0:T(8,128)S(1)}, ...), condition=%wide.region_3.4_spmd.clone.clone, body=%wide.region_2.3_spmd.sunk.clone.sunk.clone | while | flops 2228514 | bytes 4489565 | solution.py:101
  82.7 1.3 collective-permute-start.2
  84.0 4.9 %collective-permute-start.3 = (f32[1,4096]{1,0:T(1,128)S(1)}, f32[1,4096]{1,0:T(1,128)S(1)}, u32[]{:S(2)}, u32[]{:S(2)}) collective-permute-start(f32[1,4096]{1,0:T(1,128)S(1)} %get-tuple-element.964), channel_id=1, source_target_pairs={{0,1},{1,2},{2,3},{3,4},{4,5},{5,6},{6,7},{7,8},{8,9},{9,10},{10,1... | collective-permute-start | bytes 49160 | tf_op jit(solution)/shard_map/while/body/eval_jaxpr/ppermute | solution.py:22
  91.0 1.3 collective-permute-start.2
  92.3 4.9 %collective-permute-start.3 = (f32[1,4096]{1,0:T(1,128)S(1)}, f32[1,4096]{1,0:T(1,128)S(1)}, u32[]{:S(2)}, u32[]{:S(2)}) collective-permute-start(f32[1,4096]{1,0:T(1,128)S(1)} %get-tuple-element.964), channel_id=1, source_target_pairs={{0,1},{1,2},{2,3},{3,4},{4,5},{5,6},{6,7},{7,8},{8,9},{9,10},{10,1... | collective-permute-start | bytes 49160 | tf_op jit(solution)/shard_map/while/body/eval_jaxpr/ppermute | solution.py:22
  99.3 1.3 collective-permute-start.2
  100.6 5.9 %collective-permute-start.3 = (f32[1,4096]{1,0:T(1,128)S(1)}, f32[1,4096]{1,0:T(1,128)S(1)}, u32[]{:S(2)}, u32[]{:S(2)}) collective-permute-start(f32[1,4096]{1,0:T(1,128)S(1)} %get-tuple-element.964), channel_id=1, source_target_pairs={{0,1},{1,2},{2,3},{3,4},{4,5},{5,6},{6,7},{7,8},{8,9},{9,10},{10,1... | collective-permute-start | bytes 49160 | tf_op jit(solution)/shard_map/while/body/eval_jaxpr/ppermute | solution.py:22
  108.6 1.3 collective-permute-start.2
  109.9 7.0 %collective-permute-start.3 = (f32[1,4096]{1,0:T(1,128)S(1)}, f32[1,4096]{1,0:T(1,128)S(1)}, u32[]{:S(2)}, u32[]{:S(2)}) collective-permute-start(f32[1,4096]{1,0:T(1,128)S(1)} %get-tuple-element.964), channel_id=1, source_target_pairs={{0,1},{1,2},{2,3},{3,4},{4,5},{5,6},{6,7},{7,8},{8,9},{9,10},{10,1... | collective-permute-start | bytes 49160 | tf_op jit(solution)/shard_map/while/body/eval_jaxpr/ppermute | solution.py:22
  119.1 1.3 collective-permute-start.2
  120.4 7.0 %collective-permute-start.3 = (f32[1,4096]{1,0:T(1,128)S(1)}, f32[1,4096]{1,0:T(1,128)S(1)}, u32[]{:S(2)}, u32[]{:S(2)}) collective-permute-start(f32[1,4096]{1,0:T(1,128)S(1)} %get-tuple-element.964), channel_id=1, source_target_pairs={{0,1},{1,2},{2,3},{3,4},{4,5},{5,6},{6,7},{7,8},{8,9},{9,10},{10,1... | collective-permute-start | bytes 49160 | tf_op jit(solution)/shard_map/while/body/eval_jaxpr/ppermute | solution.py:22
  129.5 1.3 collective-permute-start.2
  130.8 7.0 %collective-permute-start.3 = (f32[1,4096]{1,0:T(1,128)S(1)}, f32[1,4096]{1,0:T(1,128)S(1)}, u32[]{:S(2)}, u32[]{:S(2)}) collective-permute-start(f32[1,4096]{1,0:T(1,128)S(1)} %get-tuple-element.964), channel_id=1, source_target_pairs={{0,1},{1,2},{2,3},{3,4},{4,5},{5,6},{6,7},{7,8},{8,9},{9,10},{10,1... | collective-permute-start | bytes 49160 | tf_op jit(solution)/shard_map/while/body/eval_jaxpr/ppermute | solution.py:22
  139.9 1.3 collective-permute-start.2
  141.2 7.0 %collective-permute-start.3 = (f32[1,4096]{1,0:T(1,128)S(1)}, f32[1,4096]{1,0:T(1,128)S(1)}, u32[]{:S(2)}, u32[]{:S(2)}) collective-permute-start(f32[1,4096]{1,0:T(1,128)S(1)} %get-tuple-element.964), channel_id=1, source_target_pairs={{0,1},{1,2},{2,3},{3,4},{4,5},{5,6},{6,7},{7,8},{8,9},{9,10},{10,1... | collective-permute-start | bytes 49160 | tf_op jit(solution)/shard_map/while/body/eval_jaxpr/ppermute | solution.py:22
  150.3 1.3 collective-permute-start.2
  151.6 7.0 %collective-permute-start.3 = (f32[1,4096]{1,0:T(1,128)S(1)}, f32[1,4096]{1,0:T(1,128)S(1)}, u32[]{:S(2)}, u32[]{:S(2)}) collective-permute-start(f32[1,4096]{1,0:T(1,128)S(1)} %get-tuple-element.964), channel_id=1, source_target_pairs={{0,1},{1,2},{2,3},{3,4},{4,5},{5,6},{6,7},{7,8},{8,9},{9,10},{10,1... | collective-permute-start | bytes 49160 | tf_op jit(solution)/shard_map/while/body/eval_jaxpr/ppermute | solution.py:22
  161.7 12.5 %fusion.16 = f32[16,16]{0,1:T(8,128)S(1)} fusion(f32[16,16,4096]{2,1,0:T(8,128)} %all-gather.4.cloned.1.call-done), kind=kOutput, calls=%fused_computation.38 | convolution fusion | flops 201326592 | bytes 4195328 | tf_op jit(solution)/shard_map/krc,irc->ki/dot_general | solution.py:110
  174.1 97.1 %all-gather.6.cloned.1.call-done = f32[256,4096]{1,0:T(8,128)} async-done(((f32[16,4096]{1,0:T(8,128)}), f32[256,4096]{1,0:T(8,128)}) %all-gather.6.cloned.1.call-update) | async-done | bytes 4194320 | tf_op jit(solution)/shard_map/all_gather | solution.py:107
  271.2 4.1 add.264
  275.8 9.7 %fusion.19 = f32[16,16]{0,1:T(8,128)S(1)} fusion(f32[16,16,4096]{2,1,0:T(8,128)S(1)} %copy-done, f32[16,16,4096]{2,1,0:T(8,128)S(1)} %add.264), kind=kOutput, calls=%fused_computation.39 | convolution fusion | flops 201326592 | bytes 8389632 | tf_op jit(solution)/shard_map/krc,irc->ki/dot_general | solution.py:111
  285.6 123.8 %all-reduce.4 = (f32[16,16]{0,1:T(8,128)S(1)}, f32[16,16]{0,1:T(8,128)S(1)}) all-reduce(f32[16,16]{0,1:T(8,128)S(1)} %fusion.16, f32[16,16]{0,1:T(8,128)S(1)} %fusion.19), channel_id=1, replica_groups=mesh['tm'=16,'space'=32] {'space'}, use_global_device_ids=true, to_apply=%region_5.6 | all-reduce | flops 512 | bytes 4096 | tf_op jit(solution)/shard_map/psum | solution.py:112
  409.5 1.5 cholesky.17
  412.3 27.7 %while.52 = (s32[]{:T(128)}, f32[16]{0:T(128)S(1)}, f32[16]{0:T(128)S(1)}, f32[16,16]{1,0:T(8,128)S(1)}, f32[16,16]{1,0:T(8,128)S(1)}, /*index=5*/f32[16,16]{1,0:T(8,128)S(1)}, f32[16,16]{1,0:T(8,128)S(1)}) while((s32[]{:T(128)}, f32[16]{0:T(128)S(1)}, f32[16]{0:T(128)S(1)}, f32[16,16]{1,0:T(8,128)S(1)}, ...), condition=%wide.region_9.10_spmd.clone.clone, body=%wide.region_8.9_spmd.clone.sunk.clone | while | flops 9859 | bytes 6178 | solution.py:72
  421.2 1.2 custom-call.16
  438.5 1.2 custom-call.16
  440.3 6.4 %fusion.9 = f32[1,16,4096]{2,0,1:T(1,128)S(1)} fusion(f32[16,16,4096]{2,1,0:T(8,128)} %bitcast.111, f32[16]{0:T(128)S(1)} %fusion.34), kind=kOutput, calls=%fused_computation.31 | convolution fusion | flops 12582912 | bytes 4456512 | tf_op jit(solution)/shard_map/i,irc->rc/dot_general | solution.py:115
  446.8 1.8 fusion.33
  (275 shorter events, 66.9 us)
Async XLA Ops:
  6.5 9.9 %copy-start.4 = (f32[8]{0:T(128)S(1)}, f32[8]{0:T(128)}, u32[]{:S(2)}) copy-start(f32[8]{0:T(128)} %constant.192.clone..sunk.4) | copy-start | bytes 100
  6.5 9.9 %copy-start.1 = (f32[16,4096]{1,0:T(8,128)S(1)}, f32[16,4096]{1,0:T(8,128)}, u32[]{:S(2)}) copy-start(f32[16,4096]{1,0:T(8,128)} %param.13) | copy-start | bytes 786436
  6.5 9.9 %copy-start.2 = (f32[16,4096]{1,0:T(8,128)S(1)}, f32[16,4096]{1,0:T(8,128)}, u32[]{:S(2)}) copy-start(f32[16,4096]{1,0:T(8,128)} %param.14) | copy-start | bytes 786436
  6.5 155.1 %all-gather.4.cloned.1.call-start = ((), (), s32[]{:S(2)}) async-start(), calls=%async_computation | async-start | bytes 4456448 | tf_op jit(solution)/shard_map/all_gather | solution.py:106
  7.6 5.1 %collective-permute-start.4 = (f32[1,4096]{1,0:T(1,128)S(1)}, f32[1,4096]{1,0:T(1,128)S(1)}, u32[]{:S(2)}, u32[]{:S(2)}) collective-permute-start(f32[1,4096]{1,0:T(1,128)S(1)} %get-tuple-element.749), channel_id=1, source_target_pairs={{0,1},{1,2},{2,3},{3,4},{4,5},{5,6},{6,7},{7,8},{8,9},{9,10},{10,1... | collective-permute-start | bytes 49160 | tf_op jit(solution)/shard_map/ppermute | solution.py:22
  9.3 4.4 collective-permute-start.5
  10.7 260.5 %all-gather.6.cloned.1.call-start = ((), (), s32[]{:S(2)}) async-start(), calls=%async_computation.1 | async-start | bytes 4456448 | tf_op jit(solution)/shard_map/all_gather | solution.py:107
  16.4 66.1 %copy-start.3 = (f32[1,16,4096]{2,1,0:T(8,128)S(1)}, f32[1,16,4096]{2,1,0:T(8,128)}, u32[]{:S(2)}) copy-start(f32[1,16,4096]{2,1,0:T(8,128)} %param.11) | copy-start | bytes 786436
  16.5 7.0 %collective-permute-start = (f32[1,4096]{1,0:T(1,128)S(1)}, f32[1,4096]{1,0:T(1,128)S(1)}, u32[]{:S(2)}, u32[]{:S(2)}) collective-permute-start(f32[1,4096]{1,0:T(1,128)S(1)} %get-tuple-element.936), channel_id=1, source_target_pairs={{1,0},{2,1},{3,2},{4,3},{5,4},{6,5},{7,6},{8,7},{9,8},{10,9},{11,1... | collective-permute-start | bytes 49160 | tf_op jit(solution)/shard_map/while/body/eval_jaxpr/ppermute | solution.py:23
  17.8 5.8 %collective-permute-start.1 = (f32[1,4096]{1,0:T(1,128)S(1)}, f32[1,4096]{1,0:T(1,128)S(1)}, u32[]{:S(2)}, u32[]{:S(2)}) collective-permute-start(f32[1,4096]{1,0:T(1,128)S(1)} %get-tuple-element.937), channel_id=1, source_target_pairs={{0,1},{1,2},{2,3},{3,4},{4,5},{5,6},{6,7},{7,8},{8,9},{9,10},{10,1... | collective-permute-start | bytes 49160 | tf_op jit(solution)/shard_map/while/body/eval_jaxpr/ppermute | solution.py:22
  25.0 6.3 %collective-permute-start = (f32[1,4096]{1,0:T(1,128)S(1)}, f32[1,4096]{1,0:T(1,128)S(1)}, u32[]{:S(2)}, u32[]{:S(2)}) collective-permute-start(f32[1,4096]{1,0:T(1,128)S(1)} %get-tuple-element.936), channel_id=1, source_target_pairs={{1,0},{2,1},{3,2},{4,3},{5,4},{6,5},{7,6},{8,7},{9,8},{10,9},{11,1... | collective-permute-start | bytes 49160 | tf_op jit(solution)/shard_map/while/body/eval_jaxpr/ppermute | solution.py:23
  26.3 5.1 %collective-permute-start.1 = (f32[1,4096]{1,0:T(1,128)S(1)}, f32[1,4096]{1,0:T(1,128)S(1)}, u32[]{:S(2)}, u32[]{:S(2)}) collective-permute-start(f32[1,4096]{1,0:T(1,128)S(1)} %get-tuple-element.937), channel_id=1, source_target_pairs={{0,1},{1,2},{2,3},{3,4},{4,5},{5,6},{6,7},{7,8},{8,9},{9,10},{10,1... | collective-permute-start | bytes 49160 | tf_op jit(solution)/shard_map/while/body/eval_jaxpr/ppermute | solution.py:22
  32.7 6.8 %collective-permute-start = (f32[1,4096]{1,0:T(1,128)S(1)}, f32[1,4096]{1,0:T(1,128)S(1)}, u32[]{:S(2)}, u32[]{:S(2)}) collective-permute-start(f32[1,4096]{1,0:T(1,128)S(1)} %get-tuple-element.936), channel_id=1, source_target_pairs={{1,0},{2,1},{3,2},{4,3},{5,4},{6,5},{7,6},{8,7},{9,8},{10,9},{11,1... | collective-permute-start | bytes 49160 | tf_op jit(solution)/shard_map/while/body/eval_jaxpr/ppermute | solution.py:23
  34.0 5.7 %collective-permute-start.1 = (f32[1,4096]{1,0:T(1,128)S(1)}, f32[1,4096]{1,0:T(1,128)S(1)}, u32[]{:S(2)}, u32[]{:S(2)}) collective-permute-start(f32[1,4096]{1,0:T(1,128)S(1)} %get-tuple-element.937), channel_id=1, source_target_pairs={{0,1},{1,2},{2,3},{3,4},{4,5},{5,6},{6,7},{7,8},{8,9},{9,10},{10,1... | collective-permute-start | bytes 49160 | tf_op jit(solution)/shard_map/while/body/eval_jaxpr/ppermute | solution.py:22
  41.0 6.8 %collective-permute-start = (f32[1,4096]{1,0:T(1,128)S(1)}, f32[1,4096]{1,0:T(1,128)S(1)}, u32[]{:S(2)}, u32[]{:S(2)}) collective-permute-start(f32[1,4096]{1,0:T(1,128)S(1)} %get-tuple-element.936), channel_id=1, source_target_pairs={{1,0},{2,1},{3,2},{4,3},{5,4},{6,5},{7,6},{8,7},{9,8},{10,9},{11,1... | collective-permute-start | bytes 49160 | tf_op jit(solution)/shard_map/while/body/eval_jaxpr/ppermute | solution.py:23
  42.3 5.7 %collective-permute-start.1 = (f32[1,4096]{1,0:T(1,128)S(1)}, f32[1,4096]{1,0:T(1,128)S(1)}, u32[]{:S(2)}, u32[]{:S(2)}) collective-permute-start(f32[1,4096]{1,0:T(1,128)S(1)} %get-tuple-element.937), channel_id=1, source_target_pairs={{0,1},{1,2},{2,3},{3,4},{4,5},{5,6},{6,7},{7,8},{8,9},{9,10},{10,1... | collective-permute-start | bytes 49160 | tf_op jit(solution)/shard_map/while/body/eval_jaxpr/ppermute | solution.py:22
  49.4 6.8 %collective-permute-start = (f32[1,4096]{1,0:T(1,128)S(1)}, f32[1,4096]{1,0:T(1,128)S(1)}, u32[]{:S(2)}, u32[]{:S(2)}) collective-permute-start(f32[1,4096]{1,0:T(1,128)S(1)} %get-tuple-element.936), channel_id=1, source_target_pairs={{1,0},{2,1},{3,2},{4,3},{5,4},{6,5},{7,6},{8,7},{9,8},{10,9},{11,1... | collective-permute-start | bytes 49160 | tf_op jit(solution)/shard_map/while/body/eval_jaxpr/ppermute | solution.py:23
  50.7 5.7 %collective-permute-start.1 = (f32[1,4096]{1,0:T(1,128)S(1)}, f32[1,4096]{1,0:T(1,128)S(1)}, u32[]{:S(2)}, u32[]{:S(2)}) collective-permute-start(f32[1,4096]{1,0:T(1,128)S(1)} %get-tuple-element.937), channel_id=1, source_target_pairs={{0,1},{1,2},{2,3},{3,4},{4,5},{5,6},{6,7},{7,8},{8,9},{9,10},{10,1... | collective-permute-start | bytes 49160 | tf_op jit(solution)/shard_map/while/body/eval_jaxpr/ppermute | solution.py:22
  57.7 6.8 %collective-permute-start = (f32[1,4096]{1,0:T(1,128)S(1)}, f32[1,4096]{1,0:T(1,128)S(1)}, u32[]{:S(2)}, u32[]{:S(2)}) collective-permute-start(f32[1,4096]{1,0:T(1,128)S(1)} %get-tuple-element.936), channel_id=1, source_target_pairs={{1,0},{2,1},{3,2},{4,3},{5,4},{6,5},{7,6},{8,7},{9,8},{10,9},{11,1... | collective-permute-start | bytes 49160 | tf_op jit(solution)/shard_map/while/body/eval_jaxpr/ppermute | solution.py:23
  59.0 5.7 %collective-permute-start.1 = (f32[1,4096]{1,0:T(1,128)S(1)}, f32[1,4096]{1,0:T(1,128)S(1)}, u32[]{:S(2)}, u32[]{:S(2)}) collective-permute-start(f32[1,4096]{1,0:T(1,128)S(1)} %get-tuple-element.937), channel_id=1, source_target_pairs={{0,1},{1,2},{2,3},{3,4},{4,5},{5,6},{6,7},{7,8},{8,9},{9,10},{10,1... | collective-permute-start | bytes 49160 | tf_op jit(solution)/shard_map/while/body/eval_jaxpr/ppermute | solution.py:22
  66.0 6.8 %collective-permute-start = (f32[1,4096]{1,0:T(1,128)S(1)}, f32[1,4096]{1,0:T(1,128)S(1)}, u32[]{:S(2)}, u32[]{:S(2)}) collective-permute-start(f32[1,4096]{1,0:T(1,128)S(1)} %get-tuple-element.936), channel_id=1, source_target_pairs={{1,0},{2,1},{3,2},{4,3},{5,4},{6,5},{7,6},{8,7},{9,8},{10,9},{11,1... | collective-permute-start | bytes 49160 | tf_op jit(solution)/shard_map/while/body/eval_jaxpr/ppermute | solution.py:23
  67.3 5.7 %collective-permute-start.1 = (f32[1,4096]{1,0:T(1,128)S(1)}, f32[1,4096]{1,0:T(1,128)S(1)}, u32[]{:S(2)}, u32[]{:S(2)}) collective-permute-start(f32[1,4096]{1,0:T(1,128)S(1)} %get-tuple-element.937), channel_id=1, source_target_pairs={{0,1},{1,2},{2,3},{3,4},{4,5},{5,6},{6,7},{7,8},{8,9},{9,10},{10,1... | collective-permute-start | bytes 49160 | tf_op jit(solution)/shard_map/while/body/eval_jaxpr/ppermute | solution.py:22
  74.3 6.8 %collective-permute-start = (f32[1,4096]{1,0:T(1,128)S(1)}, f32[1,4096]{1,0:T(1,128)S(1)}, u32[]{:S(2)}, u32[]{:S(2)}) collective-permute-start(f32[1,4096]{1,0:T(1,128)S(1)} %get-tuple-element.936), channel_id=1, source_target_pairs={{1,0},{2,1},{3,2},{4,3},{5,4},{6,5},{7,6},{8,7},{9,8},{10,9},{11,1... | collective-permute-start | bytes 49160 | tf_op jit(solution)/shard_map/while/body/eval_jaxpr/ppermute | solution.py:23
  75.6 5.7 %collective-permute-start.1 = (f32[1,4096]{1,0:T(1,128)S(1)}, f32[1,4096]{1,0:T(1,128)S(1)}, u32[]{:S(2)}, u32[]{:S(2)}) collective-permute-start(f32[1,4096]{1,0:T(1,128)S(1)} %get-tuple-element.937), channel_id=1, source_target_pairs={{0,1},{1,2},{2,3},{3,4},{4,5},{5,6},{6,7},{7,8},{8,9},{9,10},{10,1... | collective-permute-start | bytes 49160 | tf_op jit(solution)/shard_map/while/body/eval_jaxpr/ppermute | solution.py:22
  82.7 6.8 %collective-permute-start.2 = (f32[1,4096]{1,0:T(1,128)S(1)}, f32[1,4096]{1,0:T(1,128)S(1)}, u32[]{:S(2)}, u32[]{:S(2)}) collective-permute-start(f32[1,4096]{1,0:T(1,128)S(1)} %get-tuple-element.963), channel_id=1, source_target_pairs={{1,0},{2,1},{3,2},{4,3},{5,4},{6,5},{7,6},{8,7},{9,8},{10,9},{11,1... | collective-permute-start | bytes 49160 | tf_op jit(solution)/shard_map/while/body/eval_jaxpr/ppermute | solution.py:23
  84.0 5.7 %collective-permute-start.3 = (f32[1,4096]{1,0:T(1,128)S(1)}, f32[1,4096]{1,0:T(1,128)S(1)}, u32[]{:S(2)}, u32[]{:S(2)}) collective-permute-start(f32[1,4096]{1,0:T(1,128)S(1)} %get-tuple-element.964), channel_id=1, source_target_pairs={{0,1},{1,2},{2,3},{3,4},{4,5},{5,6},{6,7},{7,8},{8,9},{9,10},{10,1... | collective-permute-start | bytes 49160 | tf_op jit(solution)/shard_map/while/body/eval_jaxpr/ppermute | solution.py:22
  91.0 6.8 %collective-permute-start.2 = (f32[1,4096]{1,0:T(1,128)S(1)}, f32[1,4096]{1,0:T(1,128)S(1)}, u32[]{:S(2)}, u32[]{:S(2)}) collective-permute-start(f32[1,4096]{1,0:T(1,128)S(1)} %get-tuple-element.963), channel_id=1, source_target_pairs={{1,0},{2,1},{3,2},{4,3},{5,4},{6,5},{7,6},{8,7},{9,8},{10,9},{11,1... | collective-permute-start | bytes 49160 | tf_op jit(solution)/shard_map/while/body/eval_jaxpr/ppermute | solution.py:23
  92.3 5.7 %collective-permute-start.3 = (f32[1,4096]{1,0:T(1,128)S(1)}, f32[1,4096]{1,0:T(1,128)S(1)}, u32[]{:S(2)}, u32[]{:S(2)}) collective-permute-start(f32[1,4096]{1,0:T(1,128)S(1)} %get-tuple-element.964), channel_id=1, source_target_pairs={{0,1},{1,2},{2,3},{3,4},{4,5},{5,6},{6,7},{7,8},{8,9},{9,10},{10,1... | collective-permute-start | bytes 49160 | tf_op jit(solution)/shard_map/while/body/eval_jaxpr/ppermute | solution.py:22
  99.3 7.9 %collective-permute-start.2 = (f32[1,4096]{1,0:T(1,128)S(1)}, f32[1,4096]{1,0:T(1,128)S(1)}, u32[]{:S(2)}, u32[]{:S(2)}) collective-permute-start(f32[1,4096]{1,0:T(1,128)S(1)} %get-tuple-element.963), channel_id=1, source_target_pairs={{1,0},{2,1},{3,2},{4,3},{5,4},{6,5},{7,6},{8,7},{9,8},{10,9},{11,1... | collective-permute-start | bytes 49160 | tf_op jit(solution)/shard_map/while/body/eval_jaxpr/ppermute | solution.py:23
  100.6 6.7 %collective-permute-start.3 = (f32[1,4096]{1,0:T(1,128)S(1)}, f32[1,4096]{1,0:T(1,128)S(1)}, u32[]{:S(2)}, u32[]{:S(2)}) collective-permute-start(f32[1,4096]{1,0:T(1,128)S(1)} %get-tuple-element.964), channel_id=1, source_target_pairs={{0,1},{1,2},{2,3},{3,4},{4,5},{5,6},{6,7},{7,8},{8,9},{9,10},{10,1... | collective-permute-start | bytes 49160 | tf_op jit(solution)/shard_map/while/body/eval_jaxpr/ppermute | solution.py:22
  108.6 8.9 %collective-permute-start.2 = (f32[1,4096]{1,0:T(1,128)S(1)}, f32[1,4096]{1,0:T(1,128)S(1)}, u32[]{:S(2)}, u32[]{:S(2)}) collective-permute-start(f32[1,4096]{1,0:T(1,128)S(1)} %get-tuple-element.963), channel_id=1, source_target_pairs={{1,0},{2,1},{3,2},{4,3},{5,4},{6,5},{7,6},{8,7},{9,8},{10,9},{11,1... | collective-permute-start | bytes 49160 | tf_op jit(solution)/shard_map/while/body/eval_jaxpr/ppermute | solution.py:23
  109.9 7.8 %collective-permute-start.3 = (f32[1,4096]{1,0:T(1,128)S(1)}, f32[1,4096]{1,0:T(1,128)S(1)}, u32[]{:S(2)}, u32[]{:S(2)}) collective-permute-start(f32[1,4096]{1,0:T(1,128)S(1)} %get-tuple-element.964), channel_id=1, source_target_pairs={{0,1},{1,2},{2,3},{3,4},{4,5},{5,6},{6,7},{7,8},{8,9},{9,10},{10,1... | collective-permute-start | bytes 49160 | tf_op jit(solution)/shard_map/while/body/eval_jaxpr/ppermute | solution.py:22
  119.1 8.9 %collective-permute-start.2 = (f32[1,4096]{1,0:T(1,128)S(1)}, f32[1,4096]{1,0:T(1,128)S(1)}, u32[]{:S(2)}, u32[]{:S(2)}) collective-permute-start(f32[1,4096]{1,0:T(1,128)S(1)} %get-tuple-element.963), channel_id=1, source_target_pairs={{1,0},{2,1},{3,2},{4,3},{5,4},{6,5},{7,6},{8,7},{9,8},{10,9},{11,1... | collective-permute-start | bytes 49160 | tf_op jit(solution)/shard_map/while/body/eval_jaxpr/ppermute | solution.py:23
  120.4 7.8 %collective-permute-start.3 = (f32[1,4096]{1,0:T(1,128)S(1)}, f32[1,4096]{1,0:T(1,128)S(1)}, u32[]{:S(2)}, u32[]{:S(2)}) collective-permute-start(f32[1,4096]{1,0:T(1,128)S(1)} %get-tuple-element.964), channel_id=1, source_target_pairs={{0,1},{1,2},{2,3},{3,4},{4,5},{5,6},{6,7},{7,8},{8,9},{9,10},{10,1... | collective-permute-start | bytes 49160 | tf_op jit(solution)/shard_map/while/body/eval_jaxpr/ppermute | solution.py:22
  129.5 8.9 %collective-permute-start.2 = (f32[1,4096]{1,0:T(1,128)S(1)}, f32[1,4096]{1,0:T(1,128)S(1)}, u32[]{:S(2)}, u32[]{:S(2)}) collective-permute-start(f32[1,4096]{1,0:T(1,128)S(1)} %get-tuple-element.963), channel_id=1, source_target_pairs={{1,0},{2,1},{3,2},{4,3},{5,4},{6,5},{7,6},{8,7},{9,8},{10,9},{11,1... | collective-permute-start | bytes 49160 | tf_op jit(solution)/shard_map/while/body/eval_jaxpr/ppermute | solution.py:23
  130.8 7.8 %collective-permute-start.3 = (f32[1,4096]{1,0:T(1,128)S(1)}, f32[1,4096]{1,0:T(1,128)S(1)}, u32[]{:S(2)}, u32[]{:S(2)}) collective-permute-start(f32[1,4096]{1,0:T(1,128)S(1)} %get-tuple-element.964), channel_id=1, source_target_pairs={{0,1},{1,2},{2,3},{3,4},{4,5},{5,6},{6,7},{7,8},{8,9},{9,10},{10,1... | collective-permute-start | bytes 49160 | tf_op jit(solution)/shard_map/while/body/eval_jaxpr/ppermute | solution.py:22
  139.9 8.9 %collective-permute-start.2 = (f32[1,4096]{1,0:T(1,128)S(1)}, f32[1,4096]{1,0:T(1,128)S(1)}, u32[]{:S(2)}, u32[]{:S(2)}) collective-permute-start(f32[1,4096]{1,0:T(1,128)S(1)} %get-tuple-element.963), channel_id=1, source_target_pairs={{1,0},{2,1},{3,2},{4,3},{5,4},{6,5},{7,6},{8,7},{9,8},{10,9},{11,1... | collective-permute-start | bytes 49160 | tf_op jit(solution)/shard_map/while/body/eval_jaxpr/ppermute | solution.py:23
  141.2 7.8 %collective-permute-start.3 = (f32[1,4096]{1,0:T(1,128)S(1)}, f32[1,4096]{1,0:T(1,128)S(1)}, u32[]{:S(2)}, u32[]{:S(2)}) collective-permute-start(f32[1,4096]{1,0:T(1,128)S(1)} %get-tuple-element.964), channel_id=1, source_target_pairs={{0,1},{1,2},{2,3},{3,4},{4,5},{5,6},{6,7},{7,8},{8,9},{9,10},{10,1... | collective-permute-start | bytes 49160 | tf_op jit(solution)/shard_map/while/body/eval_jaxpr/ppermute | solution.py:22
  150.3 8.9 %collective-permute-start.2 = (f32[1,4096]{1,0:T(1,128)S(1)}, f32[1,4096]{1,0:T(1,128)S(1)}, u32[]{:S(2)}, u32[]{:S(2)}) collective-permute-start(f32[1,4096]{1,0:T(1,128)S(1)} %get-tuple-element.963), channel_id=1, source_target_pairs={{1,0},{2,1},{3,2},{4,3},{5,4},{6,5},{7,6},{8,7},{9,8},{10,9},{11,1... | collective-permute-start | bytes 49160 | tf_op jit(solution)/shard_map/while/body/eval_jaxpr/ppermute | solution.py:23
  151.6 7.8 %collective-permute-start.3 = (f32[1,4096]{1,0:T(1,128)S(1)}, f32[1,4096]{1,0:T(1,128)S(1)}, u32[]{:S(2)}, u32[]{:S(2)}) collective-permute-start(f32[1,4096]{1,0:T(1,128)S(1)} %get-tuple-element.964), channel_id=1, source_target_pairs={{0,1},{1,2},{2,3},{3,4},{4,5},{5,6},{6,7},{7,8},{8,9},{9,10},{10,1... | collective-permute-start | bytes 49160 | tf_op jit(solution)/shard_map/while/body/eval_jaxpr/ppermute | solution.py:22
  271.2 4.6 %copy-start = (f32[16,16,4096]{2,1,0:T(8,128)S(1)}, f32[16,16,4096]{2,1,0:T(8,128)}, u32[]{:S(2)}) copy-start(f32[16,16,4096]{2,1,0:T(8,128)} %all-gather.4.cloned.1.call-done) | copy-start | bytes 12582916
Sparse Core Ops, SparseCore 0:
  10.8 85.2 all-gather.3
  161.7 109.4 all-gather.5
where the time goes:
time: 457 us; the launch traced here: 455 us
  blocking collectives  124 us (27%)
  starting transfers between devices  113 us (25%)
  waiting for transfers between devices  101 us (22%)
  other arithmetic  53.3 us (12%)
  matrix products  35.3 us (8%)
  local copies, waits for them, and re-layouts  14.4 us (3%)
  between operations  13.6 us (3%)
    psum x1, blocking collectives, per_device(): gram_matrix, cross_matrix = lax.psum((gram_part, cross_part), 'space')  124 us
    all_gather x1, waiting for transfers between devices, per_device(): lax.all_gather(change[None], 'tm', axis=0, tiled=True)  97.1 us
    ppermute x17, starting transfers between devices, with_halo(): before = lax.ppermute(last, axis, up)  90.7 us
    ppermute x17, starting transfers between devices, with_halo(): after = lax.ppermute(leading, axis, down)  22 us
    another operation x32, other arithmetic, advance(): jax.scipy.linalg.cho_solve((factor, True), right_side)  19.7 us
    add x16, other arithmetic, relax_once(): field_now + weights[sweep_index] * (right_side - operate(field_now)) / di...  16.1 us
    dot_general x1, matrix products, per_device(): jnp.einsum('krc,irc->ki', all_starts, all_starts, precision=lax.Precision...  12.5 us
    dynamic_slice x16, local copies, waits for them, and re-layouts, relax_once(): weights[sweep_index] * (right_side - operate(field_now)) / diagonal  10.5 us
  transfers between devices with their start and end apart: 36, of which 18 were waited for; matrix products, arithmetic and copies ran while one was open for 11% of the time, Pallas kernels for 0%

commit v1 on v0

v1 whole, which is shorter than its diff:
```python
import functools
import math

import jax
import jax.numpy as jnp
from jax import lax
from jax.experimental import pallas as pl
from jax.experimental.pallas import tpu as pltpu
from jax.sharding import PartitionSpec as P

STEPS = 2
SWEEPS = 8
TAU = 0.4
LANES = 128
DEPTH = STEPS * SWEEPS
TILES = 3
VMEM = 48 * 2**20

F32 = jnp.float32
BF16 = jnp.bfloat16


def chebyshev_weights():
    return [
        1.0 / (1.0 - 0.8 * math.cos(math.pi * (2 * k + 1) / (2.0 * SWEEPS)))
        for k in range(SWEEPS)
    ]


def call(body, outs, scratch=(), smem=0, n_in=1):
    specs = [pl.BlockSpec(memory_space=pltpu.SMEM)] * smem
    specs += [pl.BlockSpec(memory_space=pltpu.VMEM)] * (n_in - smem)
    return pl.pallas_call(
        body,
        out_shape=outs,
        in_specs=specs,
        out_specs=[pl.BlockSpec(memory_space=pltpu.VMEM)] * len(outs),
        scratch_shapes=list(scratch),
        compiler_params=pltpu.CompilerParams(vmem_limit_bytes=VMEM),
    )


def pack(blocks, pos_ref, x_ref, kappa_ref, vx_ref, vy_ref, a_ref, c_ref):
    lane = lax.broadcasted_iota(jnp.int32, (DEPTH, LANES), 1)
    zero = jnp.zeros((DEPTH, LANES), F32)

    def rim(left, right):
        return jnp.where(lane < DEPTH, right, jnp.where(lane >= LANES - DEPTH, left, 0.0))

    def tile(i):
        return x_ref[:, i * LANES : (i + 1) * LANES] if 0 <= i < 2 * blocks else zero

    for t in range(blocks):
        a_ref[t, 0] = tile(2 * t)
        a_ref[t, 1] = tile(2 * t + 1)
        a_ref[t, 2] = rim(tile(2 * t - 1), tile(2 * t + 2))
    t = pos_ref[0]
    for q, ref in enumerate((kappa_ref, vx_ref, vy_ref)):
        def at(i):
            return ref[:, pl.ds(pl.multiple_of(i * LANES, LANES), LANES)]

        left = jnp.where(t > 0, at(jnp.maximum(2 * t - 1, 0)), 0.0)
        right = jnp.where(t < blocks - 1, at(jnp.minimum(2 * t + 2, 2 * blocks - 1)), 0.0)
        c_ref[q, 0] = at(2 * t)
        c_ref[q, 1] = at(2 * t + 1)
        c_ref[q, 2] = rim(left, right)


def lane_shift(tiles, lane):
    back = [pltpu.roll(v, 1, 1) for v in tiles]
    fore = [pltpu.roll(v, LANES - 1, 1) for v in tiles]
    west = [jnp.where(lane == 0, back[(c + 2) % 3], back[c]) for c in range(3)]
    east = [jnp.where(lane == LANES - 1, fore[(c + 1) % 3], fore[c]) for c in range(3)]
    return west, east


def stencil(blocks, slabs, pos_ref, up_ref, own_ref, down_ref, out_ref):
    rows = 3 * DEPTH
    t, s = pos_ref[0], pos_ref[1]
    lane = lax.broadcasted_iota(jnp.int32, (rows, LANES), 1)
    row = lax.broadcasted_iota(jnp.int32, (rows, LANES), 0) + (s - 1) * DEPTH
    inside = (row >= 0) & (row < slabs * DEPTH)

    def whole(q, c):
        return jnp.concatenate([up_ref[q, c], own_ref[q, c], down_ref[q, c]], axis=0)

    kappa = [whole(0, c) for c in range(TILES)]
    west, east = lane_shift(kappa, lane)
    for c in range(TILES):
        k, vx, vy = kappa[c], whole(1, c), whole(2, c)
        north, south = pltpu.roll(k, 1, 0), pltpu.roll(k, rows - 1, 0)
        fn, fs, fw, fe = (0.5 * (k + v) for v in (north, south, west[c], east[c]))
        inverse = 1.0 / (1.0 + TAU * (fn + fs + fw + fe))
        inverse = jnp.where(inside, inverse, 0.0)
        if c == 2:
            in_right = (lane < DEPTH) & (t < blocks - 1)
            in_left = (lane >= LANES - DEPTH) & (t > 0)
            inverse = jnp.where(in_right | in_left, inverse, 0.0)
        half = 0.5 * TAU
        values = (
            (TAU * fn + half * vy) * inverse,
            (TAU * fs - half * vy) * inverse,
            (TAU * fw + half * vx) * inverse,
            (TAU * fe - half * vx) * inverse,
            inverse,
        )
        for q, v in enumerate(values):
            for r in range(rows):
                out_ref[q, r, c] = jnp.broadcast_to(v[r : r + 1], (8, LANES))


def split(v):
    high = v.astype(BF16)
    return high, (v - high.astype(F32)).astype(BF16)


def relax(peers, up_ref, own_ref, down_ref, coef_ref, part_ref, change_ref, first_ref, field, start, right):
    n = own_ref.shape[0] // (TILES * DEPTH)
    lane = lax.broadcasted_iota(jnp.int32, (n, LANES), 1)
    weights = chebyshev_weights()
    rows = 3 * DEPTH

    def wide(q, r, c):
        v = coef_ref[q, r, c]
        return jnp.concatenate([v] * (n // 8), axis=0)

    for b, ref in enumerate((up_ref, own_ref, down_ref)):
        for r in range(DEPTH):
            for c in range(TILES):
                v = ref[pl.ds(c * DEPTH + r, n, stride=TILES * DEPTH), :]
                field[b * DEPTH + r, c] = v
                start[b * DEPTH + r, c] = v
                right[b * DEPTH + r, c] = v * wide(4, b * DEPTH + r, c)

    def sweep(k, weight):
        def one(r, north, here):
            south = [field[r + 1, c] for c in range(TILES)]
            west, east = lane_shift(here, lane)
            for c in range(TILES):
                pull = right[r, c] - here[c]
                pull += wide(0, r, c) * north[c] + wide(1, r, c) * south[c]
                pull += wide(2, r, c) * west[c] + wide(3, r, c) * east[c]
                field[r, c] = here[c] + weight * pull
            return here, south

        def two(i, carried):
            r = k + 2 * i
            north, here = carried
            north, here = one(r, north, here)
            return one(r + 1, north, here)

        lax.fori_loop(
            0,
            (rows - 2 * k) // 2,
            two,
            ([field[k - 1, c] for c in range(TILES)], [field[k, c] for c in range(TILES)]),
        )

    for step in range(STEPS):
        if step:
            done = step * SWEEPS

            def renew(r, carried):
                for c in range(TILES):
                    v = (4.0 * field[r, c] - start[r, c]) / 3.0
                    right[r, c] = v * wide(4, r, c)
                return carried

            lax.fori_loop(done + 1, rows - done - 1, renew, 0)
        for k in range(SWEEPS):
            sweep(step * SWEEPS + k + 1, weights[k])

    total = jnp.zeros((2 * n, 4 * n), F32)
    for r in range(DEPTH):
        s = jnp.concatenate([start[DEPTH + r, c] for c in range(2)], axis=1)
        e = jnp.concatenate([field[DEPTH + r, c] for c in range(2)], axis=1)
        change = e - s
        s_high, s_low = split(s)
        c_high, c_low = split(change)
        total += lax.dot_general(
            jnp.concatenate([s_high, s_low], axis=0),
            jnp.concatenate([s_high, c_high, s_low, c_low], axis=0),
            (((1,), (1,)), ((), ())),
            preferred_element_type=F32,
        )
        change_ref[:, r * 2 * LANES : (r + 1) * 2 * LANES] = jnp.concatenate([c_high, c_low], axis=0)
        first_ref[r : r + 1, :] = s[0:1]
    both = total[:n] + total[n:]
    both = both[:, : 2 * n] + both[:, 2 * n :]
    wide_both = jnp.concatenate([both] * 4, axis=1)
    lane = lax.broadcasted_iota(jnp.int32, (n, LANES), 1)
    row = lax.broadcasted_iota(jnp.int32, (n, LANES), 0)
    wide_both = jnp.where(lane // (2 * n) == row % 4, wide_both, 0.0)
    packed = [sum(wide_both[4 * q + p : 4 * q + p + 1] for p in range(4)) for q in range(n // 4)]
    packed = jnp.concatenate(packed, axis=0)
    for i in range(peers):
        part_ref[i] = packed


def add_up(peers, in_ref, out_ref):
    total = in_ref[0]
    for i in range(1, in_ref.shape[0]):
        total += in_ref[i]
    for i in range(peers):
        out_ref[i] = total


def correct(n, in_ref, change_ref, first_ref, out_ref):
    total = in_ref[0]
    for i in range(1, n):
        total += in_ref[i]
    lane = lax.broadcasted_iota(jnp.int32, (n, LANES), 1)
    row = lax.broadcasted_iota(jnp.int32, (n, LANES), 0)
    rows = jnp.concatenate([total[k // 4 : k // 4 + 1] for k in range(n)], axis=0)
    work = jnp.where(lane // (2 * n) == row % 4, rows, 0.0)
    work += pltpu.roll(work, 2 * n, 1)
    work += pltpu.roll(work, 4 * n, 1)
    for k in range(n):
        pivot = work[k : k + 1] / work[k : k + 1, k : k + 1]
        work = jnp.where(row == k, pivot, work - work[:, k : k + 1] * pivot)
    small = functools.partial(
        lax.dot_general, precision=lax.Precision.HIGHEST, preferred_element_type=F32
    )
    plain = (((1,), (0,)), ((), ()))
    lane_n = lax.broadcasted_iota(jnp.int32, (n, n), 1)
    row_n = lax.broadcasted_iota(jnp.int32, (n, n), 0)
    eye = jnp.where(lane_n == row_n, 1.0, 0.0).astype(F32)
    power = eye + small(work[:, n : 2 * n], eye, (((0,), (0,)), ((), ())))
    krylov = jnp.where((row_n == 0) & (lane_n == 0), 1.0, 0.0).astype(F32)
    step = 1
    while step < n:
        krylov += small(pltpu.roll(krylov, step, 0), power, plain)
        step *= 2
        if step < n:
            power = small(power, power, plain)
    mix = small(jnp.where(lane_n < row_n, 1.0, 0.0).astype(F32), krylov, plain)
    high, low = split(mix)
    left = jnp.concatenate(
        [jnp.concatenate([high, high], axis=1), jnp.concatenate([low, low], axis=1)], axis=0
    )
    for r in range(DEPTH):
        got = lax.dot_general(
            left,
            change_ref[:, r * 2 * LANES : (r + 1) * 2 * LANES],
            plain,
            preferred_element_type=F32,
        )
        got = got[:n] + got[n:] + first_ref[r : r + 1, :]
        for c in range(2):
            out_ref[pl.ds(c * DEPTH + r, n, stride=2 * DEPTH), :] = got[:, c * LANES : (c + 1) * LANES]


def spread(n, in_ref, out_ref):
    for i in range(2 * n):
        out_ref[:, i * LANES : (i + 1) * LANES] = in_ref[i]


def per_device(starts, kappa, velocity_x, velocity_y):
    n, slabs = lax.axis_size("tm"), lax.axis_size("space")
    pos = jnp.stack([lax.axis_index("tm"), lax.axis_index("space")]).astype(jnp.int32)
    shape = jax.ShapeDtypeStruct
    down = [(i, i + 1) for i in range(slabs - 1)]
    up = [(i + 1, i) for i in range(slabs - 1)]

    def exchange(v, axis):
        return lax.all_to_all(v, axis, 0, 0, tiled=True)

    blocks, coefs = call(
        functools.partial(pack, n),
        [shape((n, TILES, DEPTH, LANES), F32), shape((3, TILES, DEPTH, LANES), F32)],
        smem=1,
        n_in=5,
    )(pos, starts[0], kappa, velocity_x, velocity_y)
    own = exchange(blocks, "tm")
    above, below = lax.ppermute(coefs, "space", down), lax.ppermute(coefs, "space", up)
    (table,) = call(
        functools.partial(stencil, n, slabs),
        [shape((5, 3 * DEPTH, TILES, 8, LANES), F32)],
        smem=1,
        n_in=4,
    )(pos, above, coefs, below)
    own_above, own_below = lax.ppermute(own, "space", down), lax.ppermute(own, "space", up)
    flat = (n * TILES * DEPTH, LANES)
    grid = pltpu.VMEM((3 * DEPTH, TILES, n, LANES), F32)
    part, change, first = call(
        functools.partial(relax, slabs),
        [
            shape((slabs, n // 4, LANES), F32),
            shape((2 * n, DEPTH * 2 * LANES), BF16),
            shape((DEPTH, 2 * LANES), F32),
        ],
        scratch=[grid, grid, grid],
        n_in=4,
    )(own_above.reshape(flat), own.reshape(flat), own_below.reshape(flat), table)
    (part,) = call(functools.partial(add_up, n), [shape((n, n // 4, LANES), F32)])(exchange(part, "space"))
    (result,) = call(
        functools.partial(correct, n),
        [shape((n * 2 * DEPTH, LANES), F32)],
        n_in=3,
    )(exchange(part, "tm"), change, first)
    result = exchange(result.reshape(n, 2, DEPTH, LANES), "tm")
    (result,) = call(functools.partial(spread, n), [shape((DEPTH, n * 2 * LANES), F32)])(
        result.reshape(2 * n, DEPTH, LANES)
    )
    return result[None]


def solution(mesh):
    in_specs = (P("tm", "space", None), P("space", None), P("space", None), P("space", None))
    out_specs = P("tm", "space", None)
    return jax.shard_map(
        per_device, mesh=mesh, in_specs=in_specs, out_specs=out_specs, check_vma=False
    )
```

time: 457 us -> 144 us (0.32)
  starting transfers between devices: 113 us -> 9.34 us
  waiting for transfers between devices: 101 us -> 0.89 us
  other arithmetic: 53.3 us -> 0.07 us
  matrix products: 35.3 us -> 0 us
  Pallas kernels: 0 us -> 30.6 us
  blocking collectives: 124 us -> 99 us
  between operations: 13.6 us -> 0.1 us
  local copies, waits for them, and re-layouts: 14.4 us -> 3.8 us
    psum x1 -> x0, blocking collectives: 124 us -> none  [per_device(): gram_matrix, cross_matrix = lax.psum((gram_part, cross_part), 'space')]
    ppermute x34 -> x4, starting transfers between devices: 113 us -> 9.34 us  [the longest x1 3.71 us: per_device(): lax.ppermute(coefs, 'space', down)]
    all_to_all x0 -> x4, blocking collectives: none -> 99 us  [exchange(): return lax.all_to_all(v, axis, 0, 0, tiled=True)]
    all_gather x2 -> x0, waiting for transfers between devices: 97.1 us -> none  [the longest x1 97.1 us: per_device(): lax.all_gather(change[None], 'tm', axis=0, tiled=True)]
    dot_general x19 -> x0, matrix products: 30.7 us -> none  [the longest x1 12.5 us: per_device(): jnp.einsum('krc,irc->ki', all_starts, all_starts, precision=lax.Precision...]
    pallas_call x0 -> x6, Pallas kernels: none -> 30.6 us  [the longest x1 25.7 us: per_device(): call(functools.partial(relax, slabs), [shape((slabs, n // 4, LANES), F32)...]
    add x34 -> x0, other arithmetic: 21.9 us -> none  [the longest x16 16.1 us: relax_once(): field_now + weights[sweep_index] * (right_side - operate(field_now)) / di...]
    another operation x35 -> x1, other arithmetic: 21.9 us -> 0.07 us  [per_device(): jnp.stack([lax.axis_index('tm'), lax.axis_index('space')]).astype(jnp.int32)]
  transfers between devices with their start and end apart: 36 -> 4, of which waited for: 18 -> 1; matrix products, arithmetic and copies ran while one was open for 11% -> 0% of each run, Pallas kernels for 0% -> 1%
where the time goes in v1:
time: 144 us
  blocking collectives  99 us (69%)
  Pallas kernels  30.6 us (21%)
  starting transfers between devices  9.34 us (6%)
  local copies, waits for them, and re-layouts  3.8 us (3%)
    all_to_all x4, blocking collectives, exchange(): return lax.all_to_all(v, axis, 0, 0, tiled=True)  99 us
    pallas_call x1, Pallas kernels, per_device(): call(functools.partial(relax, slabs), [shape((slabs, n // 4, LANES), F32)...  25.7 us
    unnamed x8, local copies, waits for them, and re-layouts  3.8 us
    ppermute x1, starting transfers between devices, per_device(): lax.ppermute(coefs, 'space', down)  3.71 us
    ppermute x1, starting transfers between devices, per_device(): lax.ppermute(own, 'space', down)  3.05 us
  transfers between devices with their start and end apart: 4, of which 1 were waited for; matrix products, arithmetic and copies ran while one was open for 0% of the time, Pallas kernels for 1%

profile of v1, /device:TPU:32, one launch (start us, length us, event | category | flops | bytes accessed | tf_op | source)
XLA Modules:
  0.0 143.9 jit_solution(17788340240943590038)
XLA Ops:
  0.0 0.1 pad_add_fusion.pos_ref
  0.1 0.0 copy-start
  0.1 0.9 copy-done
  1.0 0.0 copy-start.1
  1.0 0.9 copy-done.1
  2.0 0.0 copy-start.2
  2.0 0.9 copy-done.2
  2.9 0.0 copy-start.3
  2.9 0.9 copy-done.3
  3.9 0.6 shard_map.46
  4.5 36.9 %all_to_all.20 = f32[16,3,16,128]{3,2,1,0:T(8,128)S(1)} all-to-all(f32[16,3,16,128]{3,2,1,0:T(8,128)S(1)} %get-tuple-element.10), channel_id=1, replica_groups=mesh['tm'=16,'space'=32] {'tm'}, dimensions={0} | all-to-all | bytes 786432 | tf_op jit(solution)/shard_map/all_to_all | solution.py:266
  41.4 1.3 collective-permute-start.1
  42.6 3.1 %collective-permute-start = (f32[16,3,16,128]{3,2,1,0:T(8,128)S(1)}, f32[16,3,16,128]{3,2,1,0:T(8,128)S(1)}, u32[]{:S(2)}, u32[]{:S(2)}) collective-permute-start(f32[16,3,16,128]{3,2,1,0:T(8,128)S(1)} %all_to_all.20), channel_id=1, source_target_pairs={{0,1},{1,2},{2,3},{3,4},{4,5},{5,6},{6,7},{7,8},{8,9},{9,10},{10,1... | collective-permute-start | bytes 1179656 | tf_op jit(solution)/shard_map/ppermute | solution.py:282
  45.7 1.3 collective-permute-start.3
  47.0 3.7 %collective-permute-start.2 = (f32[3,3,16,128]{3,2,1,0:T(8,128)S(1)}, f32[3,3,16,128]{3,2,1,0:T(8,128)S(1)}, u32[]{:S(2)}, u32[]{:S(2)}) collective-permute-start(f32[3,3,16,128]{3,2,1,0:T(8,128)S(1)} %get-tuple-element.11.own_ref), channel_id=1, source_target_pairs={{0,1},{1,2},{2,3},{3,4},{4,5},{5,6},{6,7},{7,8},{8,9},{9,10},{10,1... | collective-permute-start | bytes 221192 | tf_op jit(solution)/shard_map/ppermute | solution.py:275
  50.7 0.0 collective-permute-done.3.down_ref
  50.7 0.9 collective-permute-done.2.up_ref
  51.6 0.9 shard_map.47.coef_ref
  52.5 0.0 collective-permute-done.1
  52.5 0.0 collective-permute-done
  52.5 25.7 %shard_map.48 = (f32[32,4,128]{2,1,0:T(4,128)S(1)}, bf16[32,4096]{1,0:T(8,128)(2,1)S(1)}, f32[16,256]{1,0:T(8,128)S(1)}) custom-call(f32[768,128]{1,0:T(8,128)S(1)} %bitcast.13, f32[768,128]{1,0:T(8,128)S(1)} %bitcast.9, f32[768,128]{1,0:T(8,128)S(1)} %bitcast.12, f32[5,48,3,8,128]{4,3,2,1,0:T(8,128)S(1)} %shard_map.47.coef_ref), custom_call_target="tpu_custom_call" | custom-call | tf_op jit(solution)/shard_map/pallas_call | solution.py:285
  78.2 20.1 %all_to_all.21.in_ref = f32[32,4,128]{2,1,0:T(4,128)S(1)} all-to-all(f32[32,4,128]{2,1,0:T(4,128)S(1)} %get-tuple-element.12), channel_id=1, replica_groups=mesh['tm'=16,'space'=32] {'space'}, dimensions={0} | all-to-all | bytes 131072 | tf_op jit(solution)/shard_map/all_to_all | solution.py:266
  98.3 20.3 %all_to_all.22.in_ref = f32[16,4,128]{2,1,0:T(4,128)S(1)} all-to-all(f32[16,4,128]{2,1,0:T(4,128)S(1)} %shard_map.49), channel_id=1, replica_groups=mesh['tm'=16,'space'=32] {'tm'}, dimensions={0} | all-to-all | bytes 65536 | tf_op jit(solution)/shard_map/all_to_all | solution.py:266
  118.7 2.8 %shard_map.50 = f32[512,128]{1,0:T(8,128)S(1)} custom-call(f32[16,4,128]{2,1,0:T(4,128)S(1)} %all_to_all.22.in_ref, bf16[32,4096]{1,0:T(8,128)(2,1)S(1)} %get-tuple-element.13.change_ref, f32[16,256]{1,0:T(8,128)S(1)} %get-tuple-element.14.first_ref), custom_call_target="tpu_custom_call" | custom-call | tf_op jit(solution)/shard_map/pallas_call | solution.py:296
  121.5 21.7 %all_to_all.23 = f32[16,2,16,128]{3,2,1,0:T(8,128)S(1)} all-to-all(f32[16,2,16,128]{3,2,1,0:T(8,128)S(1)} %bitcast.10), channel_id=1, replica_groups=mesh['tm'=16,'space'=32] {'tm'}, dimensions={0} | all-to-all | bytes 524288 | tf_op jit(solution)/shard_map/all_to_all | solution.py:266
  143.2 0.7 shard_map.51
  (1 shorter events, 0.0 us)
Async XLA Ops:
  0.1 0.9 copy-start
  1.0 0.9 copy-start.1
  2.0 0.9 copy-start.2
  2.9 0.9 copy-start.3
  41.4 11.1 %collective-permute-start.1 = (f32[16,3,16,128]{3,2,1,0:T(8,128)S(1)}, f32[16,3,16,128]{3,2,1,0:T(8,128)S(1)}, u32[]{:S(2)}, u32[]{:S(2)}) collective-permute-start(f32[16,3,16,128]{3,2,1,0:T(8,128)S(1)} %all_to_all.20), channel_id=1, source_target_pairs={{1,0},{2,1},{3,2},{4,3},{5,4},{6,5},{7,6},{8,7},{9,8},{10,9},{11,1... | collective-permute-start | bytes 1179656 | tf_op jit(solution)/shard_map/ppermute | solution.py:282
  42.6 9.9 %collective-permute-start = (f32[16,3,16,128]{3,2,1,0:T(8,128)S(1)}, f32[16,3,16,128]{3,2,1,0:T(8,128)S(1)}, u32[]{:S(2)}, u32[]{:S(2)}) collective-permute-start(f32[16,3,16,128]{3,2,1,0:T(8,128)S(1)} %all_to_all.20), channel_id=1, source_target_pairs={{0,1},{1,2},{2,3},{3,4},{4,5},{5,6},{6,7},{7,8},{8,9},{9,10},{10,1... | collective-permute-start | bytes 1179656 | tf_op jit(solution)/shard_map/ppermute | solution.py:282
  45.7 5.0 %collective-permute-start.3 = (f32[3,3,16,128]{3,2,1,0:T(8,128)S(1)}, f32[3,3,16,128]{3,2,1,0:T(8,128)S(1)}, u32[]{:S(2)}, u32[]{:S(2)}) collective-permute-start(f32[3,3,16,128]{3,2,1,0:T(8,128)S(1)} %get-tuple-element.11.own_ref), channel_id=1, source_target_pairs={{1,0},{2,1},{3,2},{4,3},{5,4},{6,5},{7,6},{8,7},{9,8},{10,9},{11,1... | collective-permute-start | bytes 221192 | tf_op jit(solution)/shard_map/ppermute | solution.py:275
  47.0 4.6 %collective-permute-start.2 = (f32[3,3,16,128]{3,2,1,0:T(8,128)S(1)}, f32[3,3,16,128]{3,2,1,0:T(8,128)S(1)}, u32[]{:S(2)}, u32[]{:S(2)}) collective-permute-start(f32[3,3,16,128]{3,2,1,0:T(8,128)S(1)} %get-tuple-element.11.own_ref), channel_id=1, source_target_pairs={{0,1},{1,2},{2,3},{3,4},{4,5},{5,6},{6,7},{7,8},{8,9},{9,10},{10,1... | collective-permute-start | bytes 221192 | tf_op jit(solution)/shard_map/ppermute | solution.py:275

commit v2 on v1

--- a/solution.py
+++ b/solution.py
@@ -14,6 +14,7 @@
 LANES = 128
 DEPTH = STEPS * SWEEPS
 TILES = 3
+UNROLL = 16
 VMEM = 48 * 2**20
 
 F32 = jnp.float32
@@ -27,9 +28,10 @@
     ]
 
 
-def call(body, outs, scratch=(), smem=0, n_in=1):
+def call(body, outs, scratch=(), smem=0, hbm=0, n_in=1):
     specs = [pl.BlockSpec(memory_space=pltpu.SMEM)] * smem
-    specs += [pl.BlockSpec(memory_space=pltpu.VMEM)] * (n_in - smem)
+    specs += [pl.BlockSpec(memory_space=pltpu.HBM)] * hbm
+    specs += [pl.BlockSpec(memory_space=pltpu.VMEM)] * (n_in - smem - hbm)
     return pl.pallas_call(
         body,
         out_shape=outs,
@@ -40,30 +42,65 @@
     )
 
 
-def pack(blocks, pos_ref, x_ref, kappa_ref, vx_ref, vy_ref, a_ref, c_ref):
+BLOCK = 2 * DEPTH + 8
+
+
+def fold(rim):
+    rim = pltpu.roll(rim, DEPTH, 1)
+    return rim[:8] + pltpu.roll(rim[8:], LANES // 2, 1)
+
+
+def unfold(folded, half, lane):
+    rim = pltpu.roll(folded, (LANES - DEPTH - half * (LANES // 2)) % LANES, 1)
+    return jnp.where((lane < DEPTH) | (lane >= LANES - DEPTH), rim, 0.0)
+
+
+def pack(blocks, pos_ref, x_hbm, kappa_hbm, vx_hbm, vy_hbm, a_ref, c_ref, x_ref, f_ref, x_sem, f_sem):
     lane = lax.broadcasted_iota(jnp.int32, (DEPTH, LANES), 1)
     zero = jnp.zeros((DEPTH, LANES), F32)
-
-    def rim(left, right):
-        return jnp.where(lane < DEPTH, right, jnp.where(lane >= LANES - DEPTH, left, 0.0))
+    t = pos_ref[0]
+    tiles = 2 * blocks
+    chunks = x_sem.shape[0]
+    width = tiles * LANES // chunks
+    copies = [
+        pltpu.make_async_copy(
+            x_hbm.at[:, pl.ds(i * width, width)], x_ref.at[:, pl.ds(i * width, width)], x_sem.at[i]
+        )
+        for i in range(chunks)
+    ]
+    first = jnp.minimum(jnp.maximum(2 * t - 1, 0), tiles - 4)
+    begin = pl.multiple_of(first * LANES, LANES)
+    small = [
+        pltpu.make_async_copy(ref.at[:, pl.ds(begin, 4 * LANES)], f_ref.at[q], f_sem.at[q])
+        for q, ref in enumerate((kappa_hbm, vx_hbm, vy_hbm))
+    ]
+    for copy in copies + small:
+        copy.start()
+
+    def put(ref, i, one, two, left, right):
+        rim = jnp.where(lane < DEPTH, right, jnp.where(lane >= LANES - DEPTH, left, 0.0))
+        ref[i, :DEPTH] = one
+        ref[i, DEPTH : 2 * DEPTH] = two
+        ref[i, 2 * DEPTH :] = fold(rim)
 
     def tile(i):
-        return x_ref[:, i * LANES : (i + 1) * LANES] if 0 <= i < 2 * blocks else zero
-
-    for t in range(blocks):
-        a_ref[t, 0] = tile(2 * t)
-        a_ref[t, 1] = tile(2 * t + 1)
-        a_ref[t, 2] = rim(tile(2 * t - 1), tile(2 * t + 2))
-    t = pos_ref[0]
-    for q, ref in enumerate((kappa_ref, vx_ref, vy_ref)):
+        return x_ref[:, i * LANES : (i + 1) * LANES] if 0 <= i < tiles else zero
+
+    for copy in copies:
+        copy.wait()
+    for i in range(blocks):
+        put(a_ref, i, *(tile(2 * i + j) for j in (0, 1, -1, 2)))
+    for copy in small:
+        copy.wait()
+    for q in range(3):
+
         def at(i):
-            return ref[:, pl.ds(pl.multiple_of(i * LANES, LANES), LANES)]
-
-        left = jnp.where(t > 0, at(jnp.maximum(2 * t - 1, 0)), 0.0)
-        right = jnp.where(t < blocks - 1, at(jnp.minimum(2 * t + 2, 2 * blocks - 1)), 0.0)
-        c_ref[q, 0] = at(2 * t)
-        c_ref[q, 1] = at(2 * t + 1)
-        c_ref[q, 2] = rim(left, right)
+            i = jnp.minimum(jnp.maximum(i - first, 0), 3)
+            return f_ref[q, :, pl.ds(pl.multiple_of(i * LANES, LANES), LANES)]
+
+        left = jnp.where(t > 0, at(2 * t - 1), 0.0)
+        right = jnp.where(t < blocks - 1, at(2 * t + 2), 0.0)
+        put(c_ref, q, at(2 * t), at(2 * t + 1), left, right)
 
 
 def lane_shift(tiles, lane):
@@ -74,15 +111,21 @@
     return west, east
 
 
-def stencil(blocks, slabs, pos_ref, up_ref, own_ref, down_ref, out_ref):
+def stencil(blocks, slabs, n, pos_ref, refs, out_ref):
     rows = 3 * DEPTH
     t, s = pos_ref[0], pos_ref[1]
     lane = lax.broadcasted_iota(jnp.int32, (rows, LANES), 1)
+    lane8 = lax.broadcasted_iota(jnp.int32, (8, LANES), 1)
     row = lax.broadcasted_iota(jnp.int32, (rows, LANES), 0) + (s - 1) * DEPTH
     inside = (row >= 0) & (row < slabs * DEPTH)
 
     def whole(q, c):
-        return jnp.concatenate([up_ref[q, c], own_ref[q, c], down_ref[q, c]], axis=0)
+        base = (n + q) * BLOCK + c * DEPTH
+        if c < 2:
+            return jnp.concatenate([ref[base : base + DEPTH, :] for ref in refs], axis=0)
+        return jnp.concatenate(
+            [unfold(ref[base : base + 8, :], half, lane8) for ref in refs for half in range(2)], axis=0
+        )
 
     kappa = [whole(0, c) for c in range(TILES)]
     west, east = lane_shift(kappa, lane)
@@ -114,8 +157,9 @@
     return high, (v - high.astype(F32)).astype(BF16)
 
 
-def relax(peers, up_ref, own_ref, down_ref, coef_ref, part_ref, change_ref, first_ref, field, start, right):
-    n = own_ref.shape[0] // (TILES * DEPTH)
+def relax(n, slabs, pos_ref, up_ref, own_ref, down_ref, part_ref, change_ref, first_ref, coef_ref, field, start, right):
+    refs = (up_ref, own_ref, down_ref)
+    stencil(n, slabs, n, pos_ref, refs, coef_ref)
     lane = lax.broadcasted_iota(jnp.int32, (n, LANES), 1)
     weights = chebyshev_weights()
     rows = 3 * DEPTH
@@ -124,13 +168,19 @@
         v = coef_ref[q, r, c]
         return jnp.concatenate([v] * (n // 8), axis=0)
 
-    for b, ref in enumerate((up_ref, own_ref, down_ref)):
-        for r in range(DEPTH):
-            for c in range(TILES):
-                v = ref[pl.ds(c * DEPTH + r, n, stride=TILES * DEPTH), :]
-                field[b * DEPTH + r, c] = v
-                start[b * DEPTH + r, c] = v
-                right[b * DEPTH + r, c] = v * wide(4, b * DEPTH + r, c)
+    def begin(r, c, v):
+        field[r, c] = v
+        start[r, c] = v
+        right[r, c] = v * wide(4, r, c)
+
+    for b, ref in enumerate(refs):
+        for c in range(2):
+            for r in range(DEPTH):
+                begin(b * DEPTH + r, c, ref[pl.ds(c * DEPTH + r, n, stride=BLOCK), :])
+        for r in range(8):
+            folded = ref[pl.ds(2 * DEPTH + r, n, stride=BLOCK), :]
+            for half in range(2):
+                begin(b * DEPTH + half * 8 + r, 2, unfold(folded, half, lane))
 
     def sweep(k, weight):
         def one(r, north, here):
@@ -143,18 +193,20 @@
                 field[r, c] = here[c] + weight * pull
             return here, south
 
-        def two(i, carried):
-            r = k + 2 * i
-            north, here = carried
-            north, here = one(r, north, here)
-            return one(r + 1, north, here)
-
-        lax.fori_loop(
+        def many(i, carried):
+            for u in range(UNROLL):
+                carried = one(k + UNROLL * i + u, *carried)
+            return carried
+
+        count = rows - 2 * k
+        carried = lax.fori_loop(
             0,
-            (rows - 2 * k) // 2,
-            two,
+            count // UNROLL,
+            many,
             ([field[k - 1, c] for c in range(TILES)], [field[k, c] for c in range(TILES)]),
         )
+        for r in range(k + count // UNROLL * UNROLL, k + count):
+            carried = one(r, *carried)
 
     for step in range(STEPS):
         if step:
@@ -193,7 +245,7 @@
     wide_both = jnp.where(lane // (2 * n) == row % 4, wide_both, 0.0)
     packed = [sum(wide_both[4 * q + p : 4 * q + p + 1] for p in range(4)) for q in range(n // 4)]
     packed = jnp.concatenate(packed, axis=0)
-    for i in range(peers):
+    for i in range(slabs):
         part_ref[i] = packed
 
 
@@ -267,31 +319,31 @@
 
     blocks, coefs = call(
         functools.partial(pack, n),
-        [shape((n, TILES, DEPTH, LANES), F32), shape((3, TILES, DEPTH, LANES), F32)],
+        [shape((n, BLOCK, LANES), F32), shape((3, BLOCK, LANES), F32)],
+        scratch=[
+            pltpu.VMEM(starts.shape[1:], F32),
+            pltpu.VMEM((3, DEPTH, 4 * LANES), F32),
+            pltpu.SemaphoreType.DMA((4,)),
+            pltpu.SemaphoreType.DMA((3,)),
+        ],
         smem=1,
+        hbm=4,
         n_in=5,
     )(pos, starts[0], kappa, velocity_x, velocity_y)
-    own = exchange(blocks, "tm")
-    above, below = lax.ppermute(coefs, "space", down), lax.ppermute(coefs, "space", up)
-    (table,) = call(
-        functools.partial(stencil, n, slabs),
-        [shape((5, 3 * DEPTH, TILES, 8, LANES), F32)],
-        smem=1,
-        n_in=4,
-    )(pos, above, coefs, below)
-    own_above, own_below = lax.ppermute(own, "space", down), lax.ppermute(own, "space", up)
-    flat = (n * TILES * DEPTH, LANES)
+    own = jnp.concatenate([exchange(blocks, "tm"), coefs], axis=0).reshape((n + 3) * BLOCK, LANES)
+    above, below = lax.ppermute(own, "space", down), lax.ppermute(own, "space", up)
     grid = pltpu.VMEM((3 * DEPTH, TILES, n, LANES), F32)
     part, change, first = call(
-        functools.partial(relax, slabs),
+        functools.partial(relax, n, slabs),
         [
             shape((slabs, n // 4, LANES), F32),
             shape((2 * n, DEPTH * 2 * LANES), BF16),
             shape((DEPTH, 2 * LANES), F32),
         ],
-        scratch=[grid, grid, grid],
+        scratch=[pltpu.VMEM((5, 3 * DEPTH, TILES, 8, LANES), F32), grid, grid, grid],
+        smem=1,
         n_in=4,
-    )(own_above.reshape(flat), own.reshape(flat), own_below.reshape(flat), table)
+    )(pos, above, own, below)
     (part,) = call(functools.partial(add_up, n), [shape((n, n // 4, LANES), F32)])(exchange(part, "space"))
     (result,) = call(
         functools.partial(correct, n),

time: 144 us -> 121 us (0.84)
  Pallas kernels: 30.6 us -> 14.5 us
  starting transfers between devices: 9.34 us -> 4.35 us
  blocking collectives: 99 us -> 96.6 us
    pallas_call x3 -> x2, Pallas kernels: 27.1 us -> 10.9 us  [the longest x1 9.76 us: per_device(): call(functools.partial(relax, n, slabs), [shape((slabs, n // 4, LANES), F...]
    ppermute x2 -> x0, starting transfers between devices: 5 us -> none  [the longest x1 3.71 us: per_device(): lax.ppermute(coefs, 'space', down)]
    all_to_all x4, blocking collectives: 99 us -> 96.6 us  [exchange(): return lax.all_to_all(v, axis, 0, 0, tiled=True)]
  transfers between devices with their start and end apart: 4 -> 2, of which waited for: 1 -> 1; matrix products, arithmetic and copies ran while one was open for 0% -> 0% of each run, Pallas kernels for 1% -> 0%
where the time goes in v2:
time: 121 us
  blocking collectives  96.6 us (80%)
  Pallas kernels  14.5 us (12%)
  starting transfers between devices  4.35 us (4%)
  local copies, waits for them, and re-layouts  3.8 us (3%)
  waiting for transfers between devices  1.29 us (1%)
    all_to_all x4, blocking collectives, exchange(): return lax.all_to_all(v, axis, 0, 0, tiled=True)  96.6 us
    pallas_call x1, Pallas kernels, per_device(): call(functools.partial(relax, n, slabs), [shape((slabs, n // 4, LANES), F...  9.76 us
    unnamed x8, local copies, waits for them, and re-layouts  3.8 us
    ppermute x1, starting transfers between devices, per_device(): lax.ppermute(own, 'space', down)  3.05 us
    pallas_call x1, Pallas kernels, per_device(): call(functools.partial(correct, n), [shape((n * 2 * DEPTH, LANES), F32)],...  2.78 us
  transfers between devices with their start and end apart: 2, of which 1 were waited for; matrix products, arithmetic and copies ran while one was open for 0% of the time, Pallas kernels for 0%

profile of v2, /device:TPU:32, one launch (start us, length us, event | category | flops | bytes accessed | tf_op | source)
XLA Modules:
  0.0 120.7 jit_solution(14505027293031799859)
XLA Ops:
  0.0 0.1 pad_add_fusion.pos_ref
  0.1 0.0 copy-start
  0.1 0.9 copy-done
  1.0 0.0 copy-start.1
  1.0 0.9 copy-done.1
  2.0 0.0 copy-start.2
  2.0 0.9 copy-done.2
  2.9 0.0 copy-start.3
  2.9 0.9 copy-done.3
  3.9 1.2 shard_map.46
  5.1 35.0 %all_to_all.20 = f32[16,40,128]{2,1,0:T(8,128)S(1)} all-to-all(f32[16,40,128]{2,1,0:T(8,128)S(1)} %get-tuple-element.10), channel_id=1, replica_groups=mesh['tm'=16,'space'=32] {'tm'}, dimensions={0} | all-to-all | bytes 655360 | tf_op jit(solution)/shard_map/all_to_all | solution.py:318
  40.1 1.3 %collective-permute-start.1 = (f32[760,128]{1,0:T(8,128)S(1)}, f32[760,128]{1,0:T(8,128)S(1)}, u32[]{:S(2)}, u32[]{:S(2)}) collective-permute-start(f32[760,128]{1,0:T(8,128)S(1)} %bitcast.7), channel_id=1, source_target_pairs={{1,0},{2,1},{3,2},{4,3},{5,4},{6,5},{7,6},{8,7},{9,8},{10,9},{11,1... | collective-permute-start | bytes 1167368 | tf_op jit(solution)/shard_map/ppermute | solution.py:334
  41.4 3.1 %collective-permute-start = (f32[760,128]{1,0:T(8,128)S(1)}, f32[760,128]{1,0:T(8,128)S(1)}, u32[]{:S(2)}, u32[]{:S(2)}) collective-permute-start(f32[760,128]{1,0:T(8,128)S(1)} %bitcast.8), channel_id=1, source_target_pairs={{0,1},{1,2},{2,3},{3,4},{4,5},{5,6},{6,7},{7,8},{8,9},{9,10},{10,1... | collective-permute-start | bytes 1167368 | tf_op jit(solution)/shard_map/ppermute | solution.py:334
  44.5 0.0 collective-permute-done.1.down_ref
  44.5 1.3 %collective-permute-done.up_ref = f32[760,128]{1,0:T(8,128)S(1)} collective-permute-done((f32[760,128]{1,0:T(8,128)S(1)}, f32[760,128]{1,0:T(8,128)S(1)}, u32[]{:S(2)}, u32[]{:S(2)}) %collective-permute-start) | collective-permute-done | bytes 389152 | tf_op jit(solution)/shard_map/ppermute | solution.py:334
  45.8 9.8 %shard_map.47 = (f32[32,4,128]{2,1,0:T(4,128)S(1)}, bf16[32,4096]{1,0:T(8,128)(2,1)S(1)}, f32[16,256]{1,0:T(8,128)S(1)}) custom-call(s32[2]{0:T(128)S(1)} %pad_add_fusion.pos_ref, f32[760,128]{1,0:T(8,128)S(1)} %collective-permute-done.up_ref, f32[760,128]{1,0:T(8,128)S(1)} %bitcast.9, f32[760,128]{1,0:T(8,128)S(1)} %collective-permute-done.1.down_ref), custom_call_target="tpu_custom_call" | custom-call | tf_op jit(solution)/shard_map/pallas_call | solution.py:336
  55.5 20.9 %all_to_all.21.in_ref = f32[32,4,128]{2,1,0:T(4,128)S(1)} all-to-all(f32[32,4,128]{2,1,0:T(4,128)S(1)} %get-tuple-element.12), channel_id=1, replica_groups=mesh['tm'=16,'space'=32] {'space'}, dimensions={0} | all-to-all | bytes 131072 | tf_op jit(solution)/shard_map/all_to_all | solution.py:318
  76.5 19.0 %all_to_all.22.in_ref = f32[16,4,128]{2,1,0:T(4,128)S(1)} all-to-all(f32[16,4,128]{2,1,0:T(4,128)S(1)} %shard_map.48), channel_id=1, replica_groups=mesh['tm'=16,'space'=32] {'tm'}, dimensions={0} | all-to-all | bytes 65536 | tf_op jit(solution)/shard_map/all_to_all | solution.py:318
  95.5 2.8 %shard_map.49 = f32[512,128]{1,0:T(8,128)S(1)} custom-call(f32[16,4,128]{2,1,0:T(4,128)S(1)} %all_to_all.22.in_ref, bf16[32,4096]{1,0:T(8,128)(2,1)S(1)} %get-tuple-element.13.change_ref, f32[16,256]{1,0:T(8,128)S(1)} %get-tuple-element.14.first_ref), custom_call_target="tpu_custom_call" | custom-call | tf_op jit(solution)/shard_map/pallas_call | solution.py:348
  98.3 21.7 %all_to_all.23 = f32[16,2,16,128]{3,2,1,0:T(8,128)S(1)} all-to-all(f32[16,2,16,128]{3,2,1,0:T(8,128)S(1)} %bitcast.10), channel_id=1, replica_groups=mesh['tm'=16,'space'=32] {'tm'}, dimensions={0} | all-to-all | bytes 524288 | tf_op jit(solution)/shard_map/all_to_all | solution.py:318
  120.0 0.7 shard_map.50
  (2 shorter events, 0.1 us)
Async XLA Ops:
  0.1 0.9 copy-start
  1.0 0.9 copy-start.1
  2.0 0.9 copy-start.2
  2.9 0.9 copy-start.3
  40.1 4.4 %collective-permute-start.1 = (f32[760,128]{1,0:T(8,128)S(1)}, f32[760,128]{1,0:T(8,128)S(1)}, u32[]{:S(2)}, u32[]{:S(2)}) collective-permute-start(f32[760,128]{1,0:T(8,128)S(1)} %bitcast.7), channel_id=1, source_target_pairs={{1,0},{2,1},{3,2},{4,3},{5,4},{6,5},{7,6},{8,7},{9,8},{10,9},{11,1... | collective-permute-start | bytes 1167368 | tf_op jit(solution)/shard_map/ppermute | solution.py:334
  41.4 4.4 %collective-permute-start = (f32[760,128]{1,0:T(8,128)S(1)}, f32[760,128]{1,0:T(8,128)S(1)}, u32[]{:S(2)}, u32[]{:S(2)}) collective-permute-start(f32[760,128]{1,0:T(8,128)S(1)} %bitcast.8), channel_id=1, source_target_pairs={{0,1},{1,2},{2,3},{3,4},{4,5},{5,6},{6,7},{7,8},{8,9},{9,10},{10,1... | collective-permute-start | bytes 1167368 | tf_op jit(solution)/shard_map/ppermute | solution.py:334

commit v3 on v2

--- a/solution.py
+++ b/solution.py
@@ -14,7 +14,6 @@
 LANES = 128
 DEPTH = STEPS * SWEEPS
 TILES = 3
-UNROLL = 16
 VMEM = 48 * 2**20
 
 F32 = jnp.float32
@@ -111,7 +110,19 @@
     return west, east
 
 
-def stencil(blocks, slabs, n, pos_ref, refs, out_ref):
+def reader(pos_ref, own_ref, chip_ref, link_ref):
+    odd = lax.rem(pos_ref[1], 2) == 1
+
+    def read(b, *at):
+        if b == 1:
+            return own_ref[at]
+        pair = (chip_ref[at], link_ref[at])
+        return jnp.where(odd, *(pair if b == 0 else pair[::-1]))
+
+    return read
+
+
+def stencil(blocks, slabs, pos_ref, own_ref, chip_ref, link_ref, out_ref):
     rows = 3 * DEPTH
     t, s = pos_ref[0], pos_ref[1]
     lane = lax.broadcasted_iota(jnp.int32, (rows, LANES), 1)
@@ -119,12 +130,14 @@
     row = lax.broadcasted_iota(jnp.int32, (rows, LANES), 0) + (s - 1) * DEPTH
     inside = (row >= 0) & (row < slabs * DEPTH)
 
+    read = reader(pos_ref, own_ref, chip_ref, link_ref)
+
     def whole(q, c):
-        base = (n + q) * BLOCK + c * DEPTH
+        base = c * DEPTH
         if c < 2:
-            return jnp.concatenate([ref[base : base + DEPTH, :] for ref in refs], axis=0)
+            return jnp.concatenate([read(b, q, pl.ds(base, DEPTH)) for b in range(3)], axis=0)
         return jnp.concatenate(
-            [unfold(ref[base : base + 8, :], half, lane8) for ref in refs for half in range(2)], axis=0
+            [unfold(read(b, q, pl.ds(base, 8)), half, lane8) for b in range(3) for half in range(2)], axis=0
         )
 
     kappa = [whole(0, c) for c in range(TILES)]
@@ -157,9 +170,7 @@
     return high, (v - high.astype(F32)).astype(BF16)
 
 
-def relax(n, slabs, pos_ref, up_ref, own_ref, down_ref, part_ref, change_ref, first_ref, coef_ref, field, start, right):
-    refs = (up_ref, own_ref, down_ref)
-    stencil(n, slabs, n, pos_ref, refs, coef_ref)
+def relax(n, slabs, pos_ref, own_ref, chip_ref, link_ref, coef_ref, part_ref, change_ref, first_ref, field, start, right):
     lane = lax.broadcasted_iota(jnp.int32, (n, LANES), 1)
     weights = chebyshev_weights()
     rows = 3 * DEPTH
@@ -173,7 +184,7 @@
         start[r, c] = v
         right[r, c] = v * wide(4, r, c)
 
-    for b, ref in enumerate(refs):
+    def slab(b, ref):
         for c in range(2):
             for r in range(DEPTH):
                 begin(b * DEPTH + r, c, ref[pl.ds(c * DEPTH + r, n, stride=BLOCK), :])
@@ -181,6 +192,19 @@
             folded = ref[pl.ds(2 * DEPTH + r, n, stride=BLOCK), :]
             for half in range(2):
                 begin(b * DEPTH + half * 8 + r, 2, unfold(folded, half, lane))
+
+    odd = lax.rem(pos_ref[1], 2) == 1
+    slab(1, own_ref)
+
+    @pl.when(odd)
+    def _():
+        slab(0, chip_ref)
+        slab(2, link_ref)
+
+    @pl.when(jnp.logical_not(odd))
+    def _():
+        slab(0, link_ref)
+        slab(2, chip_ref)
 
     def sweep(k, weight):
         def one(r, north, here):
@@ -193,32 +217,18 @@
                 field[r, c] = here[c] + weight * pull
             return here, south
 
-        def many(i, carried):
-            for u in range(UNROLL):
-                carried = one(k + UNROLL * i + u, *carried)
-            return carried
-
-        count = rows - 2 * k
-        carried = lax.fori_loop(
-            0,
-            count // UNROLL,
-            many,
-            ([field[k - 1, c] for c in range(TILES)], [field[k, c] for c in range(TILES)]),
-        )
-        for r in range(k + count // UNROLL * UNROLL, k + count):
+        carried = ([field[k - 1, c] for c in range(TILES)], [field[k, c] for c in range(TILES)])
+        for r in range(k, rows - k):
             carried = one(r, *carried)
 
     for step in range(STEPS):
         if step:
             done = step * SWEEPS
 
-            def renew(r, carried):
+            for r in range(done + 1, rows - done - 1):
                 for c in range(TILES):
                     v = (4.0 * field[r, c] - start[r, c]) / 3.0
                     right[r, c] = v * wide(4, r, c)
-                return carried
-
-            lax.fori_loop(done + 1, rows - done - 1, renew, 0)
         for k in range(SWEEPS):
             sweep(step * SWEEPS + k + 1, weights[k])
 
@@ -274,18 +284,19 @@
         lax.dot_general, precision=lax.Precision.HIGHEST, preferred_element_type=F32
     )
     plain = (((1,), (0,)), ((), ()))
-    lane_n = lax.broadcasted_iota(jnp.int32, (n, n), 1)
-    row_n = lax.broadcasted_iota(jnp.int32, (n, n), 0)
-    eye = jnp.where(lane_n == row_n, 1.0, 0.0).astype(F32)
-    power = eye + small(work[:, n : 2 * n], eye, (((0,), (0,)), ((), ())))
-    krylov = jnp.where((row_n == 0) & (lane_n == 0), 1.0, 0.0).astype(F32)
+    across = (((1,), (1,)), ((), ()))
+    power = jnp.where(lane < n, pltpu.roll(work, LANES - n, 1), 0.0)
+    power += jnp.where((lane == row) | ((lane == n) & (row == 0)), 1.0, 0.0)
+    last = jnp.where((lane == n) & (row == 0), 1.0, 0.0)
+    power = jnp.concatenate([power, last], axis=0)[:, : 2 * n]
+    states = last[:, : 2 * n]
     step = 1
     while step < n:
-        krylov += small(pltpu.roll(krylov, step, 0), power, plain)
+        states += small(pltpu.roll(states, step, 0), power, across)
         step *= 2
         if step < n:
             power = small(power, power, plain)
-    mix = small(jnp.where(lane_n < row_n, 1.0, 0.0).astype(F32), krylov, plain)
+    mix = states[:, :n]
     high, low = split(mix)
     left = jnp.concatenate(
         [jnp.concatenate([high, high], axis=1), jnp.concatenate([low, low], axis=1)], axis=0
@@ -311,11 +322,14 @@
     n, slabs = lax.axis_size("tm"), lax.axis_size("space")
     pos = jnp.stack([lax.axis_index("tm"), lax.axis_index("space")]).astype(jnp.int32)
     shape = jax.ShapeDtypeStruct
-    down = [(i, i + 1) for i in range(slabs - 1)]
-    up = [(i + 1, i) for i in range(slabs - 1)]
+    chip = [(i, i ^ 1) for i in range(slabs)]
+    link = [(i, j) for i in range(slabs) if 0 <= (j := i + (1 if i % 2 else -1)) < slabs]
 
     def exchange(v, axis):
         return lax.all_to_all(v, axis, 0, 0, tiled=True)
+
+    def neighbours(v):
+        return lax.ppermute(v, "space", chip), lax.ppermute(v, "space", link)
 
     blocks, coefs = call(
         functools.partial(pack, n),
@@ -329,9 +343,17 @@
         smem=1,
         hbm=4,
         n_in=5,
-    )(pos, starts[0], kappa, velocity_x, velocity_y)
-    own = jnp.concatenate([exchange(blocks, "tm"), coefs], axis=0).reshape((n + 3) * BLOCK, LANES)
-    above, below = lax.ppermute(own, "space", down), lax.ppermute(own, "space", up)
+    )(pos, *(pltpu.with_memory_space_constraint(v, pltpu.HBM) for v in (starts[0], kappa, velocity_x, velocity_y)))
+    own = exchange(blocks, "tm").reshape(n * BLOCK, LANES)
+    coef_chip, coef_link = neighbours(coefs)
+    (table,) = call(
+        functools.partial(stencil, n, slabs),
+        [shape((5, 3 * DEPTH, TILES, 8, LANES), F32)],
+        smem=1,
+        n_in=4,
+    )(pos, coefs, coef_chip, coef_link)
+    own, table = lax.optimization_barrier((own, table))
+    own_chip, own_link = neighbours(own)
     grid = pltpu.VMEM((3 * DEPTH, TILES, n, LANES), F32)
     part, change, first = call(
         functools.partial(relax, n, slabs),
@@ -340,10 +362,10 @@
             shape((2 * n, DEPTH * 2 * LANES), BF16),
             shape((DEPTH, 2 * LANES), F32),
         ],
-        scratch=[pltpu.VMEM((5, 3 * DEPTH, TILES, 8, LANES), F32), grid, grid, grid],
+        scratch=[grid, grid, grid],
         smem=1,
-        n_in=4,
-    )(pos, above, own, below)
+        n_in=5,
+    )(pos, own, own_chip, own_link, table)
     (part,) = call(functools.partial(add_up, n), [shape((n, n // 4, LANES), F32)])(exchange(part, "space"))
     (result,) = call(
         functools.partial(correct, n),

time: 121 us -> 113 us (0.934)
  blocking collectives: 96.6 us -> 57.4 us
  starting transfers between devices: 4.35 us -> 26.2 us
  waiting for transfers between devices: 1.29 us -> 14.8 us
  local copies, waits for them, and re-layouts: 3.8 us -> 0 us
    all_to_all x4 -> x3, blocking collectives: 96.6 us -> 57.4 us  [exchange(): return lax.all_to_all(v, axis, 0, 0, tiled=True)]
    all_to_all x0 -> x1, starting transfers between devices: none -> 15.2 us  [exchange(): return lax.all_to_all(v, axis, 0, 0, tiled=True)]
    all_to_all x0 -> x1, waiting for transfers between devices: none -> 12.7 us  [exchange(): return lax.all_to_all(v, axis, 0, 0, tiled=True)]
    ppermute x2 -> x4, starting transfers between devices: 4.35 us -> 11 us  [neighbours(): return (lax.ppermute(v, 'space', chip), lax.ppermute(v, 'space', link))]
    unnamed x8 -> x0, local copies, waits for them, and re-layouts: 3.8 us -> none
    pallas_call x1, Pallas kernels: 9.76 us -> 7.55 us  [per_device(): call(functools.partial(relax, n, slabs), [shape((slabs, n // 4, LANES), F...]
    pallas_call x1, Pallas kernels: 1.17 us -> 2.48 us  [per_device(): call(functools.partial(pack, n), [shape((n, BLOCK, LANES), F32), shape((3...]
  transfers between devices with their start and end apart: 2 -> 5, of which waited for: 1 -> 3; matrix products, arithmetic and copies ran while one was open for 0% -> 0% of each run, Pallas kernels for 0% -> 1%
where the time goes in v3:
time: 113 us
  blocking collectives  57.4 us (51%)
  starting transfers between devices  26.2 us (23%)
  waiting for transfers between devices  14.8 us (13%)
  Pallas kernels  14.2 us (13%)
    all_to_all x3, blocking collectives, exchange(): return lax.all_to_all(v, axis, 0, 0, tiled=True)  57.4 us
    all_to_all x1, starting transfers between devices, exchange(): return lax.all_to_all(v, axis, 0, 0, tiled=True)  15.2 us
    all_to_all x1, waiting for transfers between devices, exchange(): return lax.all_to_all(v, axis, 0, 0, tiled=True)  12.7 us
    ppermute x4, starting transfers between devices, neighbours(): return (lax.ppermute(v, 'space', chip), lax.ppermute(v, 'space', link))  11 us
    pallas_call x1, Pallas kernels, per_device(): call(functools.partial(relax, n, slabs), [shape((slabs, n // 4, LANES), F...  7.55 us
    pallas_call x1, Pallas kernels, per_device(): call(functools.partial(correct, n), [shape((n * 2 * DEPTH, LANES), F32)],...  2.54 us
    pallas_call x1, Pallas kernels, per_device(): call(functools.partial(pack, n), [shape((n, BLOCK, LANES), F32), shape((3...  2.48 us
  transfers between devices with their start and end apart: 5, of which 3 were waited for; matrix products, arithmetic and copies ran while one was open for 0% of the time, Pallas kernels for 1%

profile of v3, /device:TPU:32, one launch (start us, length us, event | category | flops | bytes accessed | tf_op | source)
XLA Modules:
  0.0 112.8 jit_solution(4508107209085674235)
XLA Ops:
  0.0 0.1 pad_add_fusion.pos_ref
  0.1 2.5 %shard_map.46 = (f32[16,40,128]{2,1,0:T(8,128)}, f32[3,40,128]{2,1,0:T(8,128)S(1)}) custom-call(s32[2]{0:T(128)S(1)} %pad_add_fusion.pos_ref, f32[16,4096]{1,0:T(8,128)} %bitcast.12, f32[16,4096]{1,0:T(8,128)} %kappa_hbm.1, f32[16,4096]{1,0:T(8,128)} %vx_hbm.1, f32[16,4096]{1,0:T(8,128)} %vy_hbm.1), custom_call_target="tpu_custom_call" | custom-call | tf_op jit(solution)/shard_map/pallas_call | solution.py:334
  2.6 15.2 %all-to-all-start = ((f32[16,40,128]{2,1,0:T(8,128)}), f32[16,40,128]{2,1,0:T(8,128)S(1)}, u32[]{:S(2)}, u32[]{:S(2)}) async-start(f32[16,40,128]{2,1,0:T(8,128)} %get-tuple-element.12), calls=%async_computation | async-start | bytes 655360 | tf_op jit(solution)/shard_map/all_to_all | solution.py:329
  17.8 0.7 collective-permute-start.1
  18.4 4.8 %collective-permute-start = (f32[3,40,128]{2,1,0:T(8,128)S(1)}, f32[3,40,128]{2,1,0:T(8,128)S(1)}, u32[]{:S(2)}, u32[]{:S(2)}) collective-permute-start(f32[3,40,128]{2,1,0:T(8,128)S(1)} %get-tuple-element.13.own_ref), channel_id=1, source_target_pairs={{0,1},{1,0},{2,3},{3,2},{4,5},{5,4},{6,7},{7,6},{8,9},{9,8},{10,11... | collective-permute-start | bytes 184328 | tf_op jit(solution)/shard_map/ppermute | solution.py:332
  23.3 0.0 collective-permute-done.1.link_ref
  23.3 0.9 collective-permute-done.chip_ref
  24.2 0.9 shard_map.47.coef_ref
  25.1 12.7 %all-to-all-done = f32[16,40,128]{2,1,0:T(8,128)S(1)} async-done(((f32[16,40,128]{2,1,0:T(8,128)}), f32[16,40,128]{2,1,0:T(8,128)S(1)}, u32[]{:S(2)}, u32[]{:S(2)}) %all-to-all-start) | async-done | bytes 327712 | tf_op jit(solution)/shard_map/all_to_all | solution.py:329
  37.8 0.7 collective-permute-start.3
  38.5 4.8 %collective-permute-start.2 = (f32[640,128]{1,0:T(8,128)S(1)}, f32[640,128]{1,0:T(8,128)S(1)}, u32[]{:S(2)}, u32[]{:S(2)}) collective-permute-start(f32[640,128]{1,0:T(8,128)S(1)} %bitcast.8), channel_id=1, source_target_pairs={{0,1},{1,0},{2,3},{3,2},{4,5},{5,4},{6,7},{7,6},{8,9},{9,8},{10,11... | collective-permute-start | bytes 983048 | tf_op jit(solution)/shard_map/ppermute | solution.py:332
  43.3 0.0 collective-permute-done.3.link_ref
  43.3 1.2 %collective-permute-done.2.chip_ref = f32[640,128]{1,0:T(8,128)S(1)} collective-permute-done((f32[640,128]{1,0:T(8,128)S(1)}, f32[640,128]{1,0:T(8,128)S(1)}, u32[]{:S(2)}, u32[]{:S(2)}) %collective-permute-start.2) | collective-permute-done | bytes 327712 | tf_op jit(solution)/shard_map/ppermute | solution.py:332
  44.5 7.5 %shard_map.48 = (f32[32,4,128]{2,1,0:T(4,128)S(1)}, bf16[32,4096]{1,0:T(8,128)(2,1)S(1)}, f32[16,256]{1,0:T(8,128)S(1)}) custom-call(s32[2]{0:T(128)S(1)} %pad_add_fusion.pos_ref, f32[640,128]{1,0:T(8,128)S(1)} %bitcast.9, f32[640,128]{1,0:T(8,128)S(1)} %collective-permute-done.2.chip_ref, f32[640,128]{1,0:T(8,128)S(1)} %collective-permute-done.3.link_ref, ...), custom_call_target="tpu_custom_call" | custom-call | tf_op jit(solution)/shard_map/pallas_call | solution.py:358
  52.1 16.7 %all_to_all.20.in_ref = f32[32,4,128]{2,1,0:T(4,128)S(1)} all-to-all(f32[32,4,128]{2,1,0:T(4,128)S(1)} %get-tuple-element.16), channel_id=1, replica_groups=mesh['tm'=16,'space'=32] {'space'}, dimensions={0} | all-to-all | bytes 131072 | tf_op jit(solution)/shard_map/all_to_all | solution.py:329
  68.8 19.0 %all_to_all.21.in_ref = f32[16,4,128]{2,1,0:T(4,128)S(1)} all-to-all(f32[16,4,128]{2,1,0:T(4,128)S(1)} %shard_map.49), channel_id=1, replica_groups=mesh['tm'=16,'space'=32] {'tm'}, dimensions={0} | all-to-all | bytes 65536 | tf_op jit(solution)/shard_map/all_to_all | solution.py:329
  87.8 2.5 %shard_map.50 = f32[512,128]{1,0:T(8,128)S(1)} custom-call(f32[16,4,128]{2,1,0:T(4,128)S(1)} %all_to_all.21.in_ref, bf16[32,4096]{1,0:T(8,128)(2,1)S(1)} %get-tuple-element.17.change_ref, f32[16,256]{1,0:T(8,128)S(1)} %get-tuple-element.18.first_ref), custom_call_target="tpu_custom_call" | custom-call | tf_op jit(solution)/shard_map/pallas_call | solution.py:370
  90.4 21.7 %all_to_all.22 = f32[16,2,16,128]{3,2,1,0:T(8,128)S(1)} all-to-all(f32[16,2,16,128]{3,2,1,0:T(8,128)S(1)} %bitcast.10), channel_id=1, replica_groups=mesh['tm'=16,'space'=32] {'tm'}, dimensions={0} | all-to-all | bytes 524288 | tf_op jit(solution)/shard_map/all_to_all | solution.py:329
  112.1 0.7 shard_map.51
  (1 shorter events, 0.0 us)
Async XLA Ops:
  2.6 35.2 %all-to-all-start = ((f32[16,40,128]{2,1,0:T(8,128)}), f32[16,40,128]{2,1,0:T(8,128)S(1)}, u32[]{:S(2)}, u32[]{:S(2)}) async-start(f32[16,40,128]{2,1,0:T(8,128)} %get-tuple-element.12), calls=%async_computation | async-start | bytes 655360 | tf_op jit(solution)/shard_map/all_to_all | solution.py:329
  17.8 5.5 %collective-permute-start.1 = (f32[3,40,128]{2,1,0:T(8,128)S(1)}, f32[3,40,128]{2,1,0:T(8,128)S(1)}, u32[]{:S(2)}, u32[]{:S(2)}) collective-permute-start(f32[3,40,128]{2,1,0:T(8,128)S(1)} %get-tuple-element.13.own_ref), channel_id=1, source_target_pairs={{1,2},{2,1},{3,4},{4,3},{5,6},{6,5},{7,8},{8,7},{9,10},{10,9},{11,... | collective-permute-start | bytes 184328 | tf_op jit(solution)/shard_map/ppermute | solution.py:332
  18.4 5.7 %collective-permute-start = (f32[3,40,128]{2,1,0:T(8,128)S(1)}, f32[3,40,128]{2,1,0:T(8,128)S(1)}, u32[]{:S(2)}, u32[]{:S(2)}) collective-permute-start(f32[3,40,128]{2,1,0:T(8,128)S(1)} %get-tuple-element.13.own_ref), channel_id=1, source_target_pairs={{0,1},{1,0},{2,3},{3,2},{4,5},{5,4},{6,7},{7,6},{8,9},{9,8},{10,11... | collective-permute-start | bytes 184328 | tf_op jit(solution)/shard_map/ppermute | solution.py:332
  37.8 5.5 %collective-permute-start.3 = (f32[640,128]{1,0:T(8,128)S(1)}, f32[640,128]{1,0:T(8,128)S(1)}, u32[]{:S(2)}, u32[]{:S(2)}) collective-permute-start(f32[640,128]{1,0:T(8,128)S(1)} %bitcast.7), channel_id=1, source_target_pairs={{1,2},{2,1},{3,4},{4,3},{5,6},{6,5},{7,8},{8,7},{9,10},{10,9},{11,... | collective-permute-start | bytes 983048 | tf_op jit(solution)/shard_map/ppermute | solution.py:332
  38.5 6.1 %collective-permute-start.2 = (f32[640,128]{1,0:T(8,128)S(1)}, f32[640,128]{1,0:T(8,128)S(1)}, u32[]{:S(2)}, u32[]{:S(2)}) collective-permute-start(f32[640,128]{1,0:T(8,128)S(1)} %bitcast.8), channel_id=1, source_target_pairs={{0,1},{1,0},{2,3},{3,2},{4,5},{5,4},{6,7},{7,6},{8,9},{9,8},{10,11... | collective-permute-start | bytes 983048 | tf_op jit(solution)/shard_map/ppermute | solution.py:332

commit v4 on v3

--- a/solution.py
+++ b/solution.py
@@ -41,55 +41,52 @@
     )
 
 
-BLOCK = 2 * DEPTH + 8
-
-
-def fold(rim):
+BLOCK = 2 * DEPTH + 4
+COEF = 2 * DEPTH + 8
+
+
+def fold(rim, rows):
     rim = pltpu.roll(rim, DEPTH, 1)
-    return rim[:8] + pltpu.roll(rim[8:], LANES // 2, 1)
-
-
-def unfold(folded, half, lane):
-    rim = pltpu.roll(folded, (LANES - DEPTH - half * (LANES // 2)) % LANES, 1)
+    shift = LANES // 2
+    while rim.shape[0] > rows:
+        half = rim.shape[0] // 2
+        rim = rim[:half] + pltpu.roll(rim[half:], shift, 1)
+        shift //= 2
+    return rim
+
+
+def unfold(folded, shift, lane):
+    rim = pltpu.roll(folded, (LANES - DEPTH - shift) % LANES, 1)
     return jnp.where((lane < DEPTH) | (lane >= LANES - DEPTH), rim, 0.0)
 
 
-def pack(blocks, pos_ref, x_hbm, kappa_hbm, vx_hbm, vy_hbm, a_ref, c_ref, x_ref, f_ref, x_sem, f_sem):
-    lane = lax.broadcasted_iota(jnp.int32, (DEPTH, LANES), 1)
-    zero = jnp.zeros((DEPTH, LANES), F32)
+def rim(left, right, rows):
+    lane = lax.broadcasted_iota(jnp.int32, left.shape, 1)
+    return fold(jnp.where(lane < DEPTH, right, jnp.where(lane >= LANES - DEPTH, left, 0.0)), rows)
+
+
+def pack(blocks, x_ref, a_ref):
+    def tile(j):
+        inside = 0 <= j < 2 * blocks
+        return x_ref[:, j * LANES : (j + 1) * LANES] if inside else jnp.zeros((DEPTH, LANES), F32)
+
+    for k in range(blocks):
+        a_ref[k * BLOCK : k * BLOCK + DEPTH] = tile(2 * k)
+        a_ref[k * BLOCK + DEPTH : k * BLOCK + 2 * DEPTH] = tile(2 * k + 1)
+        a_ref[k * BLOCK + 2 * DEPTH : (k + 1) * BLOCK] = rim(tile(2 * k - 1), tile(2 * k + 2), 4)
+
+
+def pack_coefficients(blocks, pos_ref, kappa_hbm, vx_hbm, vy_hbm, c_ref, f_ref, f_sem):
     t = pos_ref[0]
-    tiles = 2 * blocks
-    chunks = x_sem.shape[0]
-    width = tiles * LANES // chunks
+    first = jnp.minimum(jnp.maximum(2 * t - 1, 0), 2 * blocks - 4)
+    begin = pl.multiple_of(first * LANES, LANES)
     copies = [
-        pltpu.make_async_copy(
-            x_hbm.at[:, pl.ds(i * width, width)], x_ref.at[:, pl.ds(i * width, width)], x_sem.at[i]
-        )
-        for i in range(chunks)
-    ]
-    first = jnp.minimum(jnp.maximum(2 * t - 1, 0), tiles - 4)
-    begin = pl.multiple_of(first * LANES, LANES)
-    small = [
         pltpu.make_async_copy(ref.at[:, pl.ds(begin, 4 * LANES)], f_ref.at[q], f_sem.at[q])
         for q, ref in enumerate((kappa_hbm, vx_hbm, vy_hbm))
     ]
-    for copy in copies + small:
+    for copy in copies:
         copy.start()
-
-    def put(ref, i, one, two, left, right):
-        rim = jnp.where(lane < DEPTH, right, jnp.where(lane >= LANES - DEPTH, left, 0.0))
-        ref[i, :DEPTH] = one
-        ref[i, DEPTH : 2 * DEPTH] = two
-        ref[i, 2 * DEPTH :] = fold(rim)
-
-    def tile(i):
-        return x_ref[:, i * LANES : (i + 1) * LANES] if 0 <= i < tiles else zero
-
     for copy in copies:
-        copy.wait()
-    for i in range(blocks):
-        put(a_ref, i, *(tile(2 * i + j) for j in (0, 1, -1, 2)))
-    for copy in small:
         copy.wait()
     for q in range(3):
 
@@ -97,9 +94,11 @@
             i = jnp.minimum(jnp.maximum(i - first, 0), 3)
             return f_ref[q, :, pl.ds(pl.multiple_of(i * LANES, LANES), LANES)]
 
+        c_ref[q, :DEPTH] = at(2 * t)
+        c_ref[q, DEPTH : 2 * DEPTH] = at(2 * t + 1)
         left = jnp.where(t > 0, at(2 * t - 1), 0.0)
         right = jnp.where(t < blocks - 1, at(2 * t + 2), 0.0)
-        put(c_ref, q, at(2 * t), at(2 * t + 1), left, right)
+        c_ref[q, 2 * DEPTH :] = rim(left, right, 8)
 
 
 def lane_shift(tiles, lane):
@@ -137,7 +136,7 @@
         if c < 2:
             return jnp.concatenate([read(b, q, pl.ds(base, DEPTH)) for b in range(3)], axis=0)
         return jnp.concatenate(
-            [unfold(read(b, q, pl.ds(base, 8)), half, lane8) for b in range(3) for half in range(2)], axis=0
+            [unfold(read(b, q, pl.ds(base, 8)), half * (LANES // 2), lane8) for b in range(3) for half in range(2)], axis=0
         )
 
     kappa = [whole(0, c) for c in range(TILES)]
@@ -188,10 +187,10 @@
         for c in range(2):
             for r in range(DEPTH):
                 begin(b * DEPTH + r, c, ref[pl.ds(c * DEPTH + r, n, stride=BLOCK), :])
-        for r in range(8):
+        for r in range(4):
             folded = ref[pl.ds(2 * DEPTH + r, n, stride=BLOCK), :]
-            for half in range(2):
-                begin(b * DEPTH + half * 8 + r, 2, unfold(folded, half, lane))
+            for p in range(4):
+                begin(b * DEPTH + p * 4 + r, 2, unfold(folded, p * (LANES // 4), lane))
 
     odd = lax.rem(pos_ref[1], 2) == 1
     slab(1, own_ref)
@@ -331,20 +330,16 @@
     def neighbours(v):
         return lax.ppermute(v, "space", chip), lax.ppermute(v, "space", link)
 
-    blocks, coefs = call(
-        functools.partial(pack, n),
-        [shape((n, BLOCK, LANES), F32), shape((3, BLOCK, LANES), F32)],
-        scratch=[
-            pltpu.VMEM(starts.shape[1:], F32),
-            pltpu.VMEM((3, DEPTH, 4 * LANES), F32),
-            pltpu.SemaphoreType.DMA((4,)),
-            pltpu.SemaphoreType.DMA((3,)),
-        ],
+    (blocks,) = call(functools.partial(pack, n), [shape((n * BLOCK, LANES), F32)])(starts[0])
+    own = exchange(blocks.reshape(n, BLOCK // 4, 4, LANES), "tm").reshape(n * BLOCK, LANES)
+    (coefs,) = call(
+        functools.partial(pack_coefficients, n),
+        [shape((3, COEF, LANES), F32)],
+        scratch=[pltpu.VMEM((3, DEPTH, 4 * LANES), F32), pltpu.SemaphoreType.DMA((3,))],
         smem=1,
-        hbm=4,
-        n_in=5,
-    )(pos, *(pltpu.with_memory_space_constraint(v, pltpu.HBM) for v in (starts[0], kappa, velocity_x, velocity_y)))
-    own = exchange(blocks, "tm").reshape(n * BLOCK, LANES)
+        hbm=3,
+        n_in=4,
+    )(pos, *(pltpu.with_memory_space_constraint(v, pltpu.HBM) for v in (kappa, velocity_x, velocity_y)))
     coef_chip, coef_link = neighbours(coefs)
     (table,) = call(
         functools.partial(stencil, n, slabs),

time: 113 us -> 111 us (0.982)
  waiting for transfers between devices: 14.8 us -> 11.9 us
    all_to_all x1, waiting for transfers between devices: 12.7 us -> 9.85 us  [exchange(): return lax.all_to_all(v, axis, 0, 0, tiled=True)]
    pallas_call x1 -> x2, Pallas kernels: 2.48 us -> 2.46 us  [the longest x1 1.51 us: per_device(): call(functools.partial(pack_coefficients, n), [shape((3, COEF, LANES), F3...]
  transfers between devices with their start and end apart: 5 -> 5, of which waited for: 3 -> 3; matrix products, arithmetic and copies ran while one was open for 0% -> 0% of each run, Pallas kernels for 1% -> 2%
where the time goes in v4:
time: 111 us; the launch traced here: 110 us
  blocking collectives  57 us (51%)
  starting transfers between devices  26.2 us (24%)
  Pallas kernels  14.2 us (13%)
  waiting for transfers between devices  11.9 us (11%)
    all_to_all x3, blocking collectives, exchange(): return lax.all_to_all(v, axis, 0, 0, tiled=True)  57 us
    all_to_all x1, starting transfers between devices, exchange(): return lax.all_to_all(v, axis, 0, 0, tiled=True)  15.2 us
    ppermute x4, starting transfers between devices, neighbours(): return (lax.ppermute(v, 'space', chip), lax.ppermute(v, 'space', link))  11 us
    all_to_all x1, waiting for transfers between devices, exchange(): return lax.all_to_all(v, axis, 0, 0, tiled=True)  9.85 us
    pallas_call x1, Pallas kernels, per_device(): call(functools.partial(relax, n, slabs), [shape((slabs, n // 4, LANES), F...  7.52 us
    pallas_call x1, Pallas kernels, per_device(): call(functools.partial(correct, n), [shape((n * 2 * DEPTH, LANES), F32)],...  2.54 us
  transfers between devices with their start and end apart: 5, of which 3 were waited for; matrix products, arithmetic and copies ran while one was open for 0% of the time, Pallas kernels for 2%

profile of v4, /device:TPU:32, one launch (start us, length us, event | category | flops | bytes accessed | tf_op | source)
XLA Modules:
  0.0 110.4 jit_solution(896931458439913947)
XLA Ops:
  0.0 0.0 copy-start
  0.0 0.9 copy-done
  1.0 0.9 shard_map.46
  1.9 15.2 %all-to-all-start = ((f32[16,9,4,128]{3,2,1,0:T(4,128)}), f32[16,9,4,128]{3,2,1,0:T(4,128)S(1)}, u32[]{:S(2)}, u32[]{:S(2)}) async-start(f32[16,9,4,128]{3,2,1,0:T(4,128)} %bitcast.3), calls=%async_computation | async-start | bytes 589824 | tf_op jit(solution)/shard_map/all_to_all | solution.py:328
  17.1 0.1 pad_add_fusion.pos_ref
  17.2 1.5 %shard_map.47.own_ref = f32[3,40,128]{2,1,0:T(8,128)S(1)} custom-call(s32[2]{0:T(128)S(1)} %pad_add_fusion.pos_ref, f32[16,4096]{1,0:T(8,128)} %kappa_hbm.1, f32[16,4096]{1,0:T(8,128)} %vx_hbm.1, f32[16,4096]{1,0:T(8,128)} %vy_hbm.1), custom_call_target="tpu_custom_call" | custom-call | tf_op jit(solution)/shard_map/pallas_call | solution.py:335
  18.7 0.7 collective-permute-start.1
  19.4 4.8 %collective-permute-start = (f32[3,40,128]{2,1,0:T(8,128)S(1)}, f32[3,40,128]{2,1,0:T(8,128)S(1)}, u32[]{:S(2)}, u32[]{:S(2)}) collective-permute-start(f32[3,40,128]{2,1,0:T(8,128)S(1)} %shard_map.47.own_ref), channel_id=1, source_target_pairs={{0,1},{1,0},{2,3},{3,2},{4,5},{5,4},{6,7},{7,6},{8,9},{9,8},{10,11... | collective-permute-start | bytes 184328 | tf_op jit(solution)/shard_map/ppermute | solution.py:331
  24.2 0.0 collective-permute-done.1.link_ref
  24.2 0.9 collective-permute-done.chip_ref
  25.1 0.9 shard_map.48.coef_ref
  26.0 9.8 %all-to-all-done = f32[16,9,4,128]{3,2,1,0:T(4,128)S(1)} async-done(((f32[16,9,4,128]{3,2,1,0:T(4,128)}), f32[16,9,4,128]{3,2,1,0:T(4,128)S(1)}, u32[]{:S(2)}, u32[]{:S(2)}) %all-to-all-start) | async-done | bytes 294944 | tf_op jit(solution)/shard_map/all_to_all | solution.py:328
  35.9 0.7 collective-permute-start.3
  36.5 4.8 %collective-permute-start.2 = (f32[576,128]{1,0:T(8,128)S(1)}, f32[576,128]{1,0:T(8,128)S(1)}, u32[]{:S(2)}, u32[]{:S(2)}) collective-permute-start(f32[576,128]{1,0:T(8,128)S(1)} %bitcast.9), channel_id=1, source_target_pairs={{0,1},{1,0},{2,3},{3,2},{4,5},{5,4},{6,7},{7,6},{8,9},{9,8},{10,11... | collective-permute-start | bytes 884744 | tf_op jit(solution)/shard_map/ppermute | solution.py:331
  41.4 0.0 collective-permute-done.3.link_ref
  41.4 1.2 %collective-permute-done.2.chip_ref = f32[576,128]{1,0:T(8,128)S(1)} collective-permute-done((f32[576,128]{1,0:T(8,128)S(1)}, f32[576,128]{1,0:T(8,128)S(1)}, u32[]{:S(2)}, u32[]{:S(2)}) %collective-permute-start.2) | collective-permute-done | bytes 294944 | tf_op jit(solution)/shard_map/ppermute | solution.py:331
  42.6 7.5 %shard_map.49 = (f32[32,4,128]{2,1,0:T(4,128)S(1)}, bf16[32,4096]{1,0:T(8,128)(2,1)S(1)}, f32[16,256]{1,0:T(8,128)S(1)}) custom-call(s32[2]{0:T(128)S(1)} %pad_add_fusion.pos_ref, f32[576,128]{1,0:T(8,128)S(1)} %bitcast.10, f32[576,128]{1,0:T(8,128)S(1)} %collective-permute-done.2.chip_ref, f32[576,128]{1,0:T(8,128)S(1)} %collective-permute-done.3.link_ref, ...), custom_call_target="tpu_custom_call" | custom-call | tf_op jit(solution)/shard_map/pallas_call | solution.py:353
  50.1 16.7 %all_to_all.20.in_ref = f32[32,4,128]{2,1,0:T(4,128)S(1)} all-to-all(f32[32,4,128]{2,1,0:T(4,128)S(1)} %get-tuple-element.12), channel_id=1, replica_groups=mesh['tm'=16,'space'=32] {'space'}, dimensions={0} | all-to-all | bytes 131072 | tf_op jit(solution)/shard_map/all_to_all | solution.py:328
  66.8 18.6 %all_to_all.21.in_ref = f32[16,4,128]{2,1,0:T(4,128)S(1)} all-to-all(f32[16,4,128]{2,1,0:T(4,128)S(1)} %shard_map.50), channel_id=1, replica_groups=mesh['tm'=16,'space'=32] {'tm'}, dimensions={0} | all-to-all | bytes 65536 | tf_op jit(solution)/shard_map/all_to_all | solution.py:328
  85.4 2.5 %shard_map.51 = f32[512,128]{1,0:T(8,128)S(1)} custom-call(f32[16,4,128]{2,1,0:T(4,128)S(1)} %all_to_all.21.in_ref, bf16[32,4096]{1,0:T(8,128)(2,1)S(1)} %get-tuple-element.13.change_ref, f32[16,256]{1,0:T(8,128)S(1)} %get-tuple-element.14.first_ref), custom_call_target="tpu_custom_call" | custom-call | tf_op jit(solution)/shard_map/pallas_call | solution.py:365
  88.0 21.7 %all_to_all.22 = f32[16,2,16,128]{3,2,1,0:T(8,128)S(1)} all-to-all(f32[16,2,16,128]{3,2,1,0:T(8,128)S(1)} %bitcast.11), channel_id=1, replica_groups=mesh['tm'=16,'space'=32] {'tm'}, dimensions={0} | all-to-all | bytes 524288 | tf_op jit(solution)/shard_map/all_to_all | solution.py:328
  109.7 0.7 shard_map.52
  (1 shorter events, 0.0 us)
Async XLA Ops:
  0.0 0.9 copy-start
  1.9 34.0 %all-to-all-start = ((f32[16,9,4,128]{3,2,1,0:T(4,128)}), f32[16,9,4,128]{3,2,1,0:T(4,128)S(1)}, u32[]{:S(2)}, u32[]{:S(2)}) async-start(f32[16,9,4,128]{3,2,1,0:T(4,128)} %bitcast.3), calls=%async_computation | async-start | bytes 589824 | tf_op jit(solution)/shard_map/all_to_all | solution.py:328
  18.7 5.5 %collective-permute-start.1 = (f32[3,40,128]{2,1,0:T(8,128)S(1)}, f32[3,40,128]{2,1,0:T(8,128)S(1)}, u32[]{:S(2)}, u32[]{:S(2)}) collective-permute-start(f32[3,40,128]{2,1,0:T(8,128)S(1)} %shard_map.47.own_ref), channel_id=1, source_target_pairs={{1,2},{2,1},{3,4},{4,3},{5,6},{6,5},{7,8},{8,7},{9,10},{10,9},{11,... | collective-permute-start | bytes 184328 | tf_op jit(solution)/shard_map/ppermute | solution.py:331
  19.4 5.7 %collective-permute-start = (f32[3,40,128]{2,1,0:T(8,128)S(1)}, f32[3,40,128]{2,1,0:T(8,128)S(1)}, u32[]{:S(2)}, u32[]{:S(2)}) collective-permute-start(f32[3,40,128]{2,1,0:T(8,128)S(1)} %shard_map.47.own_ref), channel_id=1, source_target_pairs={{0,1},{1,0},{2,3},{3,2},{4,5},{5,4},{6,7},{7,6},{8,9},{9,8},{10,11... | collective-permute-start | bytes 184328 | tf_op jit(solution)/shard_map/ppermute | solution.py:331
  35.9 5.5 %collective-permute-start.3 = (f32[576,128]{1,0:T(8,128)S(1)}, f32[576,128]{1,0:T(8,128)S(1)}, u32[]{:S(2)}, u32[]{:S(2)}) collective-permute-start(f32[576,128]{1,0:T(8,128)S(1)} %bitcast.8), channel_id=1, source_target_pairs={{1,2},{2,1},{3,4},{4,3},{5,6},{6,5},{7,8},{8,7},{9,10},{10,9},{11,... | collective-permute-start | bytes 884744 | tf_op jit(solution)/shard_map/ppermute | solution.py:331
  36.5 6.0 %collective-permute-start.2 = (f32[576,128]{1,0:T(8,128)S(1)}, f32[576,128]{1,0:T(8,128)S(1)}, u32[]{:S(2)}, u32[]{:S(2)}) collective-permute-start(f32[576,128]{1,0:T(8,128)S(1)} %bitcast.9), channel_id=1, source_target_pairs={{0,1},{1,0},{2,3},{3,2},{4,5},{5,4},{6,7},{7,6},{8,9},{9,8},{10,11... | collective-permute-start | bytes 884744 | tf_op jit(solution)/shard_map/ppermute | solution.py:331

commit v5 on v4

--- a/solution.py
+++ b/solution.py
@@ -65,7 +65,11 @@
     return fold(jnp.where(lane < DEPTH, right, jnp.where(lane >= LANES - DEPTH, left, 0.0)), rows)
 
 
-def pack(blocks, x_ref, a_ref):
+def pack(blocks, x_hbm, a_ref, x_ref, sem):
+    copy = pltpu.make_async_copy(x_hbm, x_ref, sem)
+    copy.start()
+    copy.wait()
+
     def tile(j):
         inside = 0 <= j < 2 * blocks
         return x_ref[:, j * LANES : (j + 1) * LANES] if inside else jnp.zeros((DEPTH, LANES), F32)
@@ -209,7 +213,7 @@
         def one(r, north, here):
             south = [field[r + 1, c] for c in range(TILES)]
             west, east = lane_shift(here, lane)
-            for c in range(TILES):
+            for c in range(TILES if k < DEPTH else 2):
                 pull = right[r, c] - here[c]
                 pull += wide(0, r, c) * north[c] + wide(1, r, c) * south[c]
                 pull += wide(2, r, c) * west[c] + wide(3, r, c) * east[c]
@@ -226,8 +230,7 @@
 
             for r in range(done + 1, rows - done - 1):
                 for c in range(TILES):
-                    v = (4.0 * field[r, c] - start[r, c]) / 3.0
-                    right[r, c] = v * wide(4, r, c)
+                    right[r, c] = (4.0 * field[r, c] - start[r, c]) * (wide(4, r, c) * (1.0 / 3.0))
         for k in range(SWEEPS):
             sweep(step * SWEEPS + k + 1, weights[k])
 
@@ -330,7 +333,12 @@
     def neighbours(v):
         return lax.ppermute(v, "space", chip), lax.ppermute(v, "space", link)
 
-    (blocks,) = call(functools.partial(pack, n), [shape((n * BLOCK, LANES), F32)])(starts[0])
+    (blocks,) = call(
+        functools.partial(pack, n),
+        [shape((n * BLOCK, LANES), F32)],
+        scratch=[pltpu.VMEM(starts.shape[1:], F32), pltpu.SemaphoreType.DMA],
+        hbm=1,
+    )(pltpu.with_memory_space_constraint(starts[0], pltpu.HBM))
     own = exchange(blocks.reshape(n, BLOCK // 4, 4, LANES), "tm").reshape(n * BLOCK, LANES)
     (coefs,) = call(
         functools.partial(pack_coefficients, n),

time: 111 us -> 111 us (level)
  no operation moved by 1% of the time
where the time goes in v5:
time: 111 us; the launch traced here: 110 us
  blocking collectives  57 us (51%)
  starting transfers between devices  26.2 us (24%)
  Pallas kernels  15.1 us (14%)
  waiting for transfers between devices  11.9 us (11%)
    all_to_all x3, blocking collectives, exchange(): return lax.all_to_all(v, axis, 0, 0, tiled=True)  57 us
    all_to_all x1, starting transfers between devices, exchange(): return lax.all_to_all(v, axis, 0, 0, tiled=True)  15.2 us
    ppermute x4, starting transfers between devices, neighbours(): return (lax.ppermute(v, 'space', chip), lax.ppermute(v, 'space', link))  11 us
    all_to_all x1, waiting for transfers between devices, exchange(): return lax.all_to_all(v, axis, 0, 0, tiled=True)  9.85 us
    pallas_call x1, Pallas kernels, per_device(): call(functools.partial(relax, n, slabs), [shape((slabs, n // 4, LANES), F...  7.5 us
    pallas_call x1, Pallas kernels, per_device(): call(functools.partial(correct, n), [shape((n * 2 * DEPTH, LANES), F32)],...  2.54 us
  transfers between devices with their start and end apart: 5, of which 3 were waited for; matrix products, arithmetic and copies ran while one was open for 0% of the time, Pallas kernels for 2%

profile of v5, /device:TPU:32, one launch (start us, length us, event | category | flops | bytes accessed | tf_op | source)
XLA Modules:
  0.0 110.4 jit_solution(11211734027986050897)
XLA Ops:
  0.0 1.9 %shard_map.46 = f32[576,128]{1,0:T(8,128)} custom-call(f32[16,4096]{1,0:T(8,128)} %bitcast.13), custom_call_target="tpu_custom_call" | custom-call | tf_op jit(solution)/shard_map/pallas_call | solution.py:336
  1.9 15.2 %all-to-all-start = ((f32[16,9,4,128]{3,2,1,0:T(4,128)}), f32[16,9,4,128]{3,2,1,0:T(4,128)S(1)}, u32[]{:S(2)}, u32[]{:S(2)}) async-start(f32[16,9,4,128]{3,2,1,0:T(4,128)} %bitcast.3), calls=%async_computation | async-start | bytes 589824 | tf_op jit(solution)/shard_map/all_to_all | solution.py:331
  17.1 0.1 pad_add_fusion.pos_ref
  17.2 1.5 %shard_map.47.own_ref = f32[3,40,128]{2,1,0:T(8,128)S(1)} custom-call(s32[2]{0:T(128)S(1)} %pad_add_fusion.pos_ref, f32[16,4096]{1,0:T(8,128)} %kappa_hbm.1, f32[16,4096]{1,0:T(8,128)} %vx_hbm.1, f32[16,4096]{1,0:T(8,128)} %vy_hbm.1), custom_call_target="tpu_custom_call" | custom-call | tf_op jit(solution)/shard_map/pallas_call | solution.py:343
  18.7 0.7 collective-permute-start.1
  19.4 4.8 %collective-permute-start = (f32[3,40,128]{2,1,0:T(8,128)S(1)}, f32[3,40,128]{2,1,0:T(8,128)S(1)}, u32[]{:S(2)}, u32[]{:S(2)}) collective-permute-start(f32[3,40,128]{2,1,0:T(8,128)S(1)} %shard_map.47.own_ref), channel_id=1, source_target_pairs={{0,1},{1,0},{2,3},{3,2},{4,5},{5,4},{6,7},{7,6},{8,9},{9,8},{10,11... | collective-permute-start | bytes 184328 | tf_op jit(solution)/shard_map/ppermute | solution.py:334
  24.3 0.0 collective-permute-done.1.link_ref
  24.3 0.9 collective-permute-done.chip_ref
  25.1 0.9 shard_map.48.coef_ref
  26.0 9.8 %all-to-all-done = f32[16,9,4,128]{3,2,1,0:T(4,128)S(1)} async-done(((f32[16,9,4,128]{3,2,1,0:T(4,128)}), f32[16,9,4,128]{3,2,1,0:T(4,128)S(1)}, u32[]{:S(2)}, u32[]{:S(2)}) %all-to-all-start) | async-done | bytes 294944 | tf_op jit(solution)/shard_map/all_to_all | solution.py:331
  35.9 0.7 collective-permute-start.3
  36.6 4.8 %collective-permute-start.2 = (f32[576,128]{1,0:T(8,128)S(1)}, f32[576,128]{1,0:T(8,128)S(1)}, u32[]{:S(2)}, u32[]{:S(2)}) collective-permute-start(f32[576,128]{1,0:T(8,128)S(1)} %bitcast.9), channel_id=1, source_target_pairs={{0,1},{1,0},{2,3},{3,2},{4,5},{5,4},{6,7},{7,6},{8,9},{9,8},{10,11... | collective-permute-start | bytes 884744 | tf_op jit(solution)/shard_map/ppermute | solution.py:334
  41.4 0.0 collective-permute-done.3.link_ref
  41.4 1.2 %collective-permute-done.2.chip_ref = f32[576,128]{1,0:T(8,128)S(1)} collective-permute-done((f32[576,128]{1,0:T(8,128)S(1)}, f32[576,128]{1,0:T(8,128)S(1)}, u32[]{:S(2)}, u32[]{:S(2)}) %collective-permute-start.2) | collective-permute-done | bytes 294944 | tf_op jit(solution)/shard_map/ppermute | solution.py:334
  42.6 7.5 %shard_map.49 = (f32[32,4,128]{2,1,0:T(4,128)S(1)}, bf16[32,4096]{1,0:T(8,128)(2,1)S(1)}, f32[16,256]{1,0:T(8,128)S(1)}) custom-call(s32[2]{0:T(128)S(1)} %pad_add_fusion.pos_ref, f32[576,128]{1,0:T(8,128)S(1)} %bitcast.10, f32[576,128]{1,0:T(8,128)S(1)} %collective-permute-done.2.chip_ref, f32[576,128]{1,0:T(8,128)S(1)} %collective-permute-done.3.link_ref, ...), custom_call_target="tpu_custom_call" | custom-call | tf_op jit(solution)/shard_map/pallas_call | solution.py:361
  50.1 16.7 %all_to_all.20.in_ref = f32[32,4,128]{2,1,0:T(4,128)S(1)} all-to-all(f32[32,4,128]{2,1,0:T(4,128)S(1)} %get-tuple-element.12), channel_id=1, replica_groups=mesh['tm'=16,'space'=32] {'space'}, dimensions={0} | all-to-all | bytes 131072 | tf_op jit(solution)/shard_map/all_to_all | solution.py:331
  66.8 18.6 %all_to_all.21.in_ref = f32[16,4,128]{2,1,0:T(4,128)S(1)} all-to-all(f32[16,4,128]{2,1,0:T(4,128)S(1)} %shard_map.50), channel_id=1, replica_groups=mesh['tm'=16,'space'=32] {'tm'}, dimensions={0} | all-to-all | bytes 65536 | tf_op jit(solution)/shard_map/all_to_all | solution.py:331
  85.4 2.5 %shard_map.51 = f32[512,128]{1,0:T(8,128)S(1)} custom-call(f32[16,4,128]{2,1,0:T(4,128)S(1)} %all_to_all.21.in_ref, bf16[32,4096]{1,0:T(8,128)(2,1)S(1)} %get-tuple-element.13.change_ref, f32[16,256]{1,0:T(8,128)S(1)} %get-tuple-element.14.first_ref), custom_call_target="tpu_custom_call" | custom-call | tf_op jit(solution)/shard_map/pallas_call | solution.py:373
  88.0 21.7 %all_to_all.22 = f32[16,2,16,128]{3,2,1,0:T(8,128)S(1)} all-to-all(f32[16,2,16,128]{3,2,1,0:T(8,128)S(1)} %bitcast.11), channel_id=1, replica_groups=mesh['tm'=16,'space'=32] {'tm'}, dimensions={0} | all-to-all | bytes 524288 | tf_op jit(solution)/shard_map/all_to_all | solution.py:331
  109.7 0.7 shard_map.52
  (1 shorter events, 0.0 us)
Async XLA Ops:
  1.9 34.0 %all-to-all-start = ((f32[16,9,4,128]{3,2,1,0:T(4,128)}), f32[16,9,4,128]{3,2,1,0:T(4,128)S(1)}, u32[]{:S(2)}, u32[]{:S(2)}) async-start(f32[16,9,4,128]{3,2,1,0:T(4,128)} %bitcast.3), calls=%async_computation | async-start | bytes 589824 | tf_op jit(solution)/shard_map/all_to_all | solution.py:331
  18.7 5.5 %collective-permute-start.1 = (f32[3,40,128]{2,1,0:T(8,128)S(1)}, f32[3,40,128]{2,1,0:T(8,128)S(1)}, u32[]{:S(2)}, u32[]{:S(2)}) collective-permute-start(f32[3,40,128]{2,1,0:T(8,128)S(1)} %shard_map.47.own_ref), channel_id=1, source_target_pairs={{1,2},{2,1},{3,4},{4,3},{5,6},{6,5},{7,8},{8,7},{9,10},{10,9},{11,... | collective-permute-start | bytes 184328 | tf_op jit(solution)/shard_map/ppermute | solution.py:334
  19.4 5.7 %collective-permute-start = (f32[3,40,128]{2,1,0:T(8,128)S(1)}, f32[3,40,128]{2,1,0:T(8,128)S(1)}, u32[]{:S(2)}, u32[]{:S(2)}) collective-permute-start(f32[3,40,128]{2,1,0:T(8,128)S(1)} %shard_map.47.own_ref), channel_id=1, source_target_pairs={{0,1},{1,0},{2,3},{3,2},{4,5},{5,4},{6,7},{7,6},{8,9},{9,8},{10,11... | collective-permute-start | bytes 184328 | tf_op jit(solution)/shard_map/ppermute | solution.py:334
  35.9 5.5 %collective-permute-start.3 = (f32[576,128]{1,0:T(8,128)S(1)}, f32[576,128]{1,0:T(8,128)S(1)}, u32[]{:S(2)}, u32[]{:S(2)}) collective-permute-start(f32[576,128]{1,0:T(8,128)S(1)} %bitcast.8), channel_id=1, source_target_pairs={{1,2},{2,1},{3,4},{4,3},{5,6},{6,5},{7,8},{8,7},{9,10},{10,9},{11,... | collective-permute-start | bytes 884744 | tf_op jit(solution)/shard_map/ppermute | solution.py:334
  36.6 6.0 %collective-permute-start.2 = (f32[576,128]{1,0:T(8,128)S(1)}, f32[576,128]{1,0:T(8,128)S(1)}, u32[]{:S(2)}, u32[]{:S(2)}) collective-permute-start(f32[576,128]{1,0:T(8,128)S(1)} %bitcast.9), channel_id=1, source_target_pairs={{0,1},{1,0},{2,3},{3,2},{4,5},{5,4},{6,7},{7,6},{8,9},{9,8},{10,11... | collective-permute-start | bytes 884744 | tf_op jit(solution)/shard_map/ppermute | solution.py:334
